TPU v7x, 512 devices: a whole 4x4x16 slice. The times are simulated.
512 devices in a mesh: row: 16 (over z), col: 8 (over y, x_hi), rep: 4 (over x_lo, core).
Axes of the slice: x: 4 (x_hi: 2, x_lo: 2; x = x_hi * 2 + x_lo), y: 4, z: 16, core: 2. Of those that a mesh axis runs over, the one named last changes fastest.
Arguments:
- image_acts: bfloat16 [32768, 1152], P(('row', 'col', 'rep')), may hold values from -320 to 320, as said below
- text_acts: bfloat16 [32768, 1152], P(('row', 'col', 'rep')), may hold values from -320 to 320, as said below
- image_gain: float32 [1152], replicated, may hold values from 0.1 to 1.9
- image_offset: float32 [1152], replicated, may hold values from -3 to 3
- text_gain: float32 [1152], replicated, may hold values from 0.1 to 1.9
- text_offset: float32 [1152], replicated, may hold values from -3 to 3
Outputs:
- image_grad: bfloat16 [32768, 1152], P(('row', 'col', 'rep'))
- text_grad: bfloat16 [32768, 1152], P(('row', 'col', 'rep'))
Inputs may be any that keep to these rules, and one draw needn't show every extreme that they name: `image_acts`: cached activations of the image tower. `text_acts`: cached activations of the text tower.
All inputs are finite; a program needn't handle non-finite values.
Results may differ from a plain program's by a relative error of at most 0.0081.
Values may be sent and summed in bfloat16 or wider, within the bound.
No kernel may reach another device: no remote copies, remote signals or barrier semaphores. Data moves between devices by JAX's collectives and lax.ppermute only.
A program may use at most 64 MiB of HBM per device.

v0:
```python
import jax
import jax.numpy as jnp
from jax import lax
from jax.sharding import PartitionSpec as P

logit_scale = 10.0
logit_shift = -10.0
loss_weight = 16.0
norm_eps = 1e-06
unit_eps = 1e-06


def from_behind(value, axis, steps):
    count = lax.axis_size(axis)
    pairs = [(source, (source + steps) % count) for source in range(count)]
    return lax.ppermute(value, axis, pairs)


def normalize(acts, gains, offset):
    values = acts.astype(jnp.float32)
    row_mean = jnp.mean(values, axis=-1, keepdims=True)
    centered = values - row_mean
    row_var = jnp.mean(centered * centered, axis=-1, keepdims=True)
    inverse_std = lax.rsqrt(row_var + norm_eps)
    hat_rows = centered * inverse_std
    scaled = hat_rows * gains + offset
    inverse_len = lax.rsqrt(jnp.sum(scaled * scaled, axis=-1, keepdims=True) + unit_eps)
    return (scaled * inverse_len, hat_rows, inverse_std, inverse_len)


def norm_backward(unit_grad, unit_rows, hat_rows, inverse_std, inverse_len, gains):
    along = jnp.sum(unit_rows * unit_grad, axis=-1, keepdims=True)
    grad_scaled = (unit_grad - unit_rows * along) * inverse_len
    grad_hat = grad_scaled * gains
    mean_one = jnp.mean(grad_hat, axis=-1, keepdims=True)
    mean_two = jnp.mean(grad_hat * hat_rows, axis=-1, keepdims=True)
    return inverse_std * (grad_hat - mean_one - hat_rows * mean_two)


def pair_labels(fixed_rows, moving_rows, first_col, first_visit):
    fixed_index = lax.broadcasted_iota(jnp.int32, (fixed_rows, moving_rows), 0)
    moving_index = lax.broadcasted_iota(jnp.int32, (fixed_rows, moving_rows), 1) + first_col
    hit = jnp.logical_and(fixed_index == moving_index, first_visit)
    return jnp.where(hit, jnp.float32(1.0), jnp.float32(0.0))


def tile_pass(fixed_block, moving, image_partial, carried, labels):
    scores = lax.dot_general(
        fixed_block, moving, (((1,), (1,)), ((), ())), preferred_element_type=jnp.float32
    )
    pair_grad = (
        loss_weight * (jax.nn.sigmoid(logit_scale * scores + logit_shift) - labels)
    ).astype(jnp.bfloat16)
    image_partial = image_partial + logit_scale * jnp.dot(
        pair_grad, moving, preferred_element_type=jnp.float32
    )
    carried = carried + logit_scale * lax.dot_general(
        pair_grad, fixed_block, (((0,), (0,)), ((), ())), preferred_element_type=jnp.float32
    )
    return (image_partial, carried)


def shift_ahead(moving, carried):
    moving = from_behind(moving, "row", 1)
    carried = from_behind(carried, "row", 1)
    return (moving, carried)


def send_home_ahead(carried):
    return from_behind(carried, "row", 1)


def body(image_acts, text_acts, image_gain, image_offset, text_gain, text_offset):
    image_unit, image_hat, image_std, image_len = normalize(image_acts, image_gain, image_offset)
    text_unit, text_hat, text_std, text_len = normalize(text_acts, text_gain, text_offset)
    own_image = image_unit.astype(jnp.bfloat16)
    own_text = text_unit.astype(jnp.bfloat16)
    fixed_block = lax.all_gather(own_image, "col", axis=0, tiled=True)
    group_rows = own_text.shape[0]
    width = own_text.shape[1]
    fixed_rows = fixed_block.shape[0]
    cycle_length = lax.axis_size("row")
    diag_start = lax.axis_index("col") * group_rows
    image_partial = jnp.zeros((fixed_rows, width), jnp.float32)

    def ahead_step(position, cycle_state):
        moving, carried, partial_sum = cycle_state
        labels = pair_labels(fixed_rows, group_rows, diag_start, position == 0)
        partial_sum, carried = tile_pass(fixed_block, moving, partial_sum, carried, labels)
        moving, carried = shift_ahead(moving, carried)
        return (moving, carried, partial_sum)

    start_state = (own_text, jnp.zeros((group_rows, width), jnp.float32), image_partial)
    moving, carried, image_partial = lax.fori_loop(0, cycle_length - 1, ahead_step, start_state)
    labels = pair_labels(fixed_rows, group_rows, diag_start, cycle_length == 1)
    image_partial, carried = tile_pass(fixed_block, moving, image_partial, carried, labels)
    text_unit_grad = send_home_ahead(carried)
    text_grad = norm_backward(text_unit_grad, text_unit, text_hat, text_std, text_len, text_gain)
    image_unit_grad = lax.psum_scatter(image_partial, "col", scatter_dimension=0, tiled=True)
    image_grad = norm_backward(
        image_unit_grad, image_unit, image_hat, image_std, image_len, image_gain
    )
    return (image_grad.astype(jnp.bfloat16), text_grad.astype(jnp.bfloat16))


def solution(mesh):
    placed = (P(("row", "col", "rep"), None), P(("row", "col", "rep"), None), P(), P(), P(), P())
    return jax.shard_map(
        body,
        mesh=mesh,
        in_specs=placed,
        out_specs=(P(("row", "col", "rep"), None), P(("row", "col", "rep"), None)),
        check_vma=False,
    )
```

profile of v0, /device:TPU:32, one launch (start us, length us, event | category | flops | bytes accessed | tf_op | source)
XLA Modules:
  0.0 469.5 jit_solution(1553088674955216003)
XLA Ops:
  17.5 61.6 %all-gather.2.cloned.1.call-done = bf16[512,1152]{1,0:T(8,128)(2,1)} async-done(((bf16[64,1152]{1,0:T(8,128)(2,1)}), bf16[512,1152]{1,0:T(8,128)(2,1)}) %all-gather.2.cloned.1.call-update) | async-done | bytes 1179664 | tf_op jit(solution)/shard_map/all_gather | solution.py:78
  79.9 288.0 %while.18 = (s32[]{:T(128)}, bf16[64,1152]{1,0:T(8,128)(2,1)}, f32[64,1152]{1,0:T(8,128)}, f32[512,1152]{1,0:T(8,128)S(1)}, bf16[512,1152]{1,0:T(8,128)(2,1)}, /*index=5*/s32[]{:T(128)}, s32[]{:T(128)}, s32[]{:T(128)}) while((s32[]{:T(128)}, bf16[64,1152]{1,0:T(8,128)(2,1)}, f32[64,1152]{1,0:T(8,128)}, f32[512,1152]{1,0:T(8,128)S(1)}, ...), condition=%wide.region_7.8_spmd.clone, body=%wide.region_6.7_spmd.clone.sunk | while | flops 228769856 | bytes 16122604 | solution.py:94
  81.5 3.5 collective-permute-start
  89.4 3.5 collective-permute-start.1
  94.7 4.0 collective-permute-done.1
  101.0 3.8 collective-permute-start
  109.3 4.3 collective-permute-start.1
  120.5 4.7 collective-permute-start
  129.6 4.3 collective-permute-start.1
  140.8 4.3 collective-permute-start
  149.4 3.5 collective-permute-start.1
  154.7 3.5 collective-permute-done.1
  160.7 3.5 collective-permute-start
  168.5 3.8 collective-permute-start.1
  174.2 3.2 collective-permute-done.1
  179.7 4.0 collective-permute-start
  188.1 4.3 collective-permute-start.1
  199.3 4.3 collective-permute-start
  208.0 3.6 collective-permute-start.1
  213.4 3.4 collective-permute-done.1
  219.2 3.6 collective-permute-start
  227.2 3.1 collective-permute-start.1
  232.2 3.9 collective-permute-done.1
  238.4 3.1 collective-permute-start
  246.0 3.1 collective-permute-start.1
  250.9 3.9 collective-permute-done.1
  257.2 3.1 collective-permute-start
  264.7 3.1 collective-permute-start.1
  269.6 3.9 collective-permute-done.1
  275.9 3.1 collective-permute-start
  283.4 3.1 collective-permute-start.1
  288.4 3.9 collective-permute-done.1
  294.6 3.1 collective-permute-start
  302.2 3.1 collective-permute-start.1
  307.1 3.9 collective-permute-done.1
  313.4 3.1 collective-permute-start
  320.9 3.1 collective-permute-start.1
  325.8 3.9 collective-permute-done.1
  332.1 3.1 collective-permute-start
  339.6 3.1 collective-permute-start.1
  344.6 3.9 collective-permute-done.1
  350.8 3.1 collective-permute-start
  358.4 3.1 collective-permute-start.1
  363.3 3.9 collective-permute-done.1
  369.7 2.8 fusion.11
  374.2 3.1 collective-permute-start.2
  377.3 5.5 %collective-permute-done.2 = f32[64,1152]{1,0:T(8,128)S(1)} collective-permute-done((f32[64,1152]{1,0:T(8,128)S(1)}, f32[64,1152]{1,0:T(8,128)S(1)}, u32[]{:S(2)}, u32[]{:S(2)}) %collective-permute-start.2) | collective-permute-done | bytes 294944 | tf_op jit(solution)/shard_map/ppermute | solution.py:16
  384.2 75.1 %reduce-scatter.2.cloned.1.call-done = f32[64,1152]{1,0:T(8,128)} async-done(((f32[512,1152]{1,0:T(8,128)}), f32[64,1152]{1,0:T(8,128)}) %reduce-scatter.2.cloned.1.call-update) | async-done | bytes 294928 | tf_op jit(solution)/shard_map/reduce_scatter | solution.py:99
  (207 shorter events, 155.6 us)
Async XLA Ops:
  7.2 72.0 %all-gather.2.cloned.1.call-start = ((), (), s32[]{:S(2)}) async-start(), calls=%async_computation.1 | async-start | bytes 1327104 | tf_op jit(solution)/shard_map/all_gather | solution.py:78
  12.4 446.9 %reduce-scatter.2.cloned.1.call-start = ((), (), s32[]{:S(2)}) async-start(), calls=%async_computation.2 | async-start | bytes 2654208 | tf_op jit(solution)/shard_map/reduce_scatter | solution.py:99
  15.8 64.1 %copy-start.12 = (f32[64]{0:T(128)}, f32[64]{0:T(128)S(1)}, u32[]{:S(2)}) copy-start(f32[64]{0:T(128)S(1)} %add_rsqrt_fusion.1) | copy-start | bytes 772
  81.5 13.1 %collective-permute-start = (bf16[64,1152]{1,0:T(8,128)(2,1)}, bf16[64,1152]{1,0:T(8,128)(2,1)}, u32[]{:S(2)}, u32[]{:S(2)}) collective-permute-start(bf16[64,1152]{1,0:T(8,128)(2,1)} %copy.13), channel_id=1, source_target_pairs={{0,32},{32,64},{64,96},{96,128},{128,160},{160,192},{192,224},{224... | collective-permute-start | bytes 442376 | tf_op jit(solution)/shard_map/while/body/eval_jaxpr/ppermute | solution.py:16
  89.4 9.2 %collective-permute-start.1 = (f32[64,1152]{1,0:T(8,128)}, f32[64,1152]{1,0:T(8,128)S(1)}, u32[]{:S(2)}, u32[]{:S(2)}) collective-permute-start(f32[64,1152]{1,0:T(8,128)} %fusion.80), channel_id=1, source_target_pairs={{0,32},{32,64},{64,96},{96,128},{128,160},{160,192},{192,224},{224... | collective-permute-start | bytes 884744 | tf_op jit(solution)/shard_map/while/body/eval_jaxpr/ppermute | solution.py:16
  99.4 7.9 %copy-start = (bf16[512,1152]{1,0:T(8,128)(2,1)S(1)}, bf16[512,1152]{1,0:T(8,128)(2,1)}, u32[]{:S(2)}) copy-start(bf16[512,1152]{1,0:T(8,128)(2,1)} %get-tuple-element.216) | copy-start | bytes 3538948 | tf_op jit(solution)/shard_map/while
  101.0 14.3 %collective-permute-start = (bf16[64,1152]{1,0:T(8,128)(2,1)}, bf16[64,1152]{1,0:T(8,128)(2,1)}, u32[]{:S(2)}, u32[]{:S(2)}) collective-permute-start(bf16[64,1152]{1,0:T(8,128)(2,1)} %copy.13), channel_id=1, source_target_pairs={{0,32},{32,64},{64,96},{96,128},{128,160},{160,192},{192,224},{224... | collective-permute-start | bytes 442376 | tf_op jit(solution)/shard_map/while/body/eval_jaxpr/ppermute | solution.py:16
  109.3 8.8 %collective-permute-start.1 = (f32[64,1152]{1,0:T(8,128)}, f32[64,1152]{1,0:T(8,128)S(1)}, u32[]{:S(2)}, u32[]{:S(2)}) collective-permute-start(f32[64,1152]{1,0:T(8,128)} %fusion.80), channel_id=1, source_target_pairs={{0,32},{32,64},{64,96},{96,128},{128,160},{160,192},{192,224},{224... | collective-permute-start | bytes 884744 | tf_op jit(solution)/shard_map/while/body/eval_jaxpr/ppermute | solution.py:16
  118.8 8.7 %copy-start = (bf16[512,1152]{1,0:T(8,128)(2,1)S(1)}, bf16[512,1152]{1,0:T(8,128)(2,1)}, u32[]{:S(2)}) copy-start(bf16[512,1152]{1,0:T(8,128)(2,1)} %get-tuple-element.216) | copy-start | bytes 3538948 | tf_op jit(solution)/shard_map/while
  120.5 15.1 %collective-permute-start = (bf16[64,1152]{1,0:T(8,128)(2,1)}, bf16[64,1152]{1,0:T(8,128)(2,1)}, u32[]{:S(2)}, u32[]{:S(2)}) collective-permute-start(bf16[64,1152]{1,0:T(8,128)(2,1)} %copy.13), channel_id=1, source_target_pairs={{0,32},{32,64},{64,96},{96,128},{128,160},{160,192},{192,224},{224... | collective-permute-start | bytes 442376 | tf_op jit(solution)/shard_map/while/body/eval_jaxpr/ppermute | solution.py:16
  129.6 8.8 %collective-permute-start.1 = (f32[64,1152]{1,0:T(8,128)}, f32[64,1152]{1,0:T(8,128)S(1)}, u32[]{:S(2)}, u32[]{:S(2)}) collective-permute-start(f32[64,1152]{1,0:T(8,128)} %fusion.80), channel_id=1, source_target_pairs={{0,32},{32,64},{64,96},{96,128},{128,160},{160,192},{192,224},{224... | collective-permute-start | bytes 884744 | tf_op jit(solution)/shard_map/while/body/eval_jaxpr/ppermute | solution.py:16
  139.1 8.3 %copy-start = (bf16[512,1152]{1,0:T(8,128)(2,1)S(1)}, bf16[512,1152]{1,0:T(8,128)(2,1)}, u32[]{:S(2)}) copy-start(bf16[512,1152]{1,0:T(8,128)(2,1)} %get-tuple-element.216) | copy-start | bytes 3538948 | tf_op jit(solution)/shard_map/while
  140.8 13.9 %collective-permute-start = (bf16[64,1152]{1,0:T(8,128)(2,1)}, bf16[64,1152]{1,0:T(8,128)(2,1)}, u32[]{:S(2)}, u32[]{:S(2)}) collective-permute-start(bf16[64,1152]{1,0:T(8,128)(2,1)} %copy.13), channel_id=1, source_target_pairs={{0,32},{32,64},{64,96},{96,128},{128,160},{160,192},{192,224},{224... | collective-permute-start | bytes 442376 | tf_op jit(solution)/shard_map/while/body/eval_jaxpr/ppermute | solution.py:16
  149.4 8.8 %collective-permute-start.1 = (f32[64,1152]{1,0:T(8,128)}, f32[64,1152]{1,0:T(8,128)S(1)}, u32[]{:S(2)}, u32[]{:S(2)}) collective-permute-start(f32[64,1152]{1,0:T(8,128)} %fusion.80), channel_id=1, source_target_pairs={{0,32},{32,64},{64,96},{96,128},{128,160},{160,192},{192,224},{224... | collective-permute-start | bytes 884744 | tf_op jit(solution)/shard_map/while/body/eval_jaxpr/ppermute | solution.py:16
  160.7 13.5 %collective-permute-start = (bf16[64,1152]{1,0:T(8,128)(2,1)}, bf16[64,1152]{1,0:T(8,128)(2,1)}, u32[]{:S(2)}, u32[]{:S(2)}) collective-permute-start(bf16[64,1152]{1,0:T(8,128)(2,1)} %copy.13), channel_id=1, source_target_pairs={{0,32},{32,64},{64,96},{96,128},{128,160},{160,192},{192,224},{224... | collective-permute-start | bytes 442376 | tf_op jit(solution)/shard_map/while/body/eval_jaxpr/ppermute | solution.py:16
  168.5 8.8 %collective-permute-start.1 = (f32[64,1152]{1,0:T(8,128)}, f32[64,1152]{1,0:T(8,128)S(1)}, u32[]{:S(2)}, u32[]{:S(2)}) collective-permute-start(f32[64,1152]{1,0:T(8,128)} %fusion.80), channel_id=1, source_target_pairs={{0,32},{32,64},{64,96},{96,128},{128,160},{160,192},{192,224},{224... | collective-permute-start | bytes 884744 | tf_op jit(solution)/shard_map/while/body/eval_jaxpr/ppermute | solution.py:16
  178.0 8.0 %copy-start = (bf16[512,1152]{1,0:T(8,128)(2,1)S(1)}, bf16[512,1152]{1,0:T(8,128)(2,1)}, u32[]{:S(2)}) copy-start(bf16[512,1152]{1,0:T(8,128)(2,1)} %get-tuple-element.216) | copy-start | bytes 3538948 | tf_op jit(solution)/shard_map/while
  179.7 14.4 %collective-permute-start = (bf16[64,1152]{1,0:T(8,128)(2,1)}, bf16[64,1152]{1,0:T(8,128)(2,1)}, u32[]{:S(2)}, u32[]{:S(2)}) collective-permute-start(bf16[64,1152]{1,0:T(8,128)(2,1)} %copy.13), channel_id=1, source_target_pairs={{0,32},{32,64},{64,96},{96,128},{128,160},{160,192},{192,224},{224... | collective-permute-start | bytes 442376 | tf_op jit(solution)/shard_map/while/body/eval_jaxpr/ppermute | solution.py:16
  188.1 8.8 %collective-permute-start.1 = (f32[64,1152]{1,0:T(8,128)}, f32[64,1152]{1,0:T(8,128)S(1)}, u32[]{:S(2)}, u32[]{:S(2)}) collective-permute-start(f32[64,1152]{1,0:T(8,128)} %fusion.80), channel_id=1, source_target_pairs={{0,32},{32,64},{64,96},{96,128},{128,160},{160,192},{192,224},{224... | collective-permute-start | bytes 884744 | tf_op jit(solution)/shard_map/while/body/eval_jaxpr/ppermute | solution.py:16
  197.6 8.3 %copy-start = (bf16[512,1152]{1,0:T(8,128)(2,1)S(1)}, bf16[512,1152]{1,0:T(8,128)(2,1)}, u32[]{:S(2)}) copy-start(bf16[512,1152]{1,0:T(8,128)(2,1)} %get-tuple-element.216) | copy-start | bytes 3538948 | tf_op jit(solution)/shard_map/while
  199.3 14.1 %collective-permute-start = (bf16[64,1152]{1,0:T(8,128)(2,1)}, bf16[64,1152]{1,0:T(8,128)(2,1)}, u32[]{:S(2)}, u32[]{:S(2)}) collective-permute-start(bf16[64,1152]{1,0:T(8,128)(2,1)} %copy.13), channel_id=1, source_target_pairs={{0,32},{32,64},{64,96},{96,128},{128,160},{160,192},{192,224},{224... | collective-permute-start | bytes 442376 | tf_op jit(solution)/shard_map/while/body/eval_jaxpr/ppermute | solution.py:16
  208.0 8.8 %collective-permute-start.1 = (f32[64,1152]{1,0:T(8,128)}, f32[64,1152]{1,0:T(8,128)S(1)}, u32[]{:S(2)}, u32[]{:S(2)}) collective-permute-start(f32[64,1152]{1,0:T(8,128)} %fusion.80), channel_id=1, source_target_pairs={{0,32},{32,64},{64,96},{96,128},{128,160},{160,192},{192,224},{224... | collective-permute-start | bytes 884744 | tf_op jit(solution)/shard_map/while/body/eval_jaxpr/ppermute | solution.py:16
  217.5 7.7 %copy-start = (bf16[512,1152]{1,0:T(8,128)(2,1)S(1)}, bf16[512,1152]{1,0:T(8,128)(2,1)}, u32[]{:S(2)}) copy-start(bf16[512,1152]{1,0:T(8,128)(2,1)} %get-tuple-element.216) | copy-start | bytes 3538948 | tf_op jit(solution)/shard_map/while
  219.2 13.0 %collective-permute-start = (bf16[64,1152]{1,0:T(8,128)(2,1)}, bf16[64,1152]{1,0:T(8,128)(2,1)}, u32[]{:S(2)}, u32[]{:S(2)}) collective-permute-start(bf16[64,1152]{1,0:T(8,128)(2,1)} %copy.13), channel_id=1, source_target_pairs={{0,32},{32,64},{64,96},{96,128},{128,160},{160,192},{192,224},{224... | collective-permute-start | bytes 442376 | tf_op jit(solution)/shard_map/while/body/eval_jaxpr/ppermute | solution.py:16
  227.2 8.8 %collective-permute-start.1 = (f32[64,1152]{1,0:T(8,128)}, f32[64,1152]{1,0:T(8,128)S(1)}, u32[]{:S(2)}, u32[]{:S(2)}) collective-permute-start(f32[64,1152]{1,0:T(8,128)} %fusion.80), channel_id=1, source_target_pairs={{0,32},{32,64},{64,96},{96,128},{128,160},{160,192},{192,224},{224... | collective-permute-start | bytes 884744 | tf_op jit(solution)/shard_map/while/body/eval_jaxpr/ppermute | solution.py:16
  238.4 12.4 %collective-permute-start = (bf16[64,1152]{1,0:T(8,128)(2,1)}, bf16[64,1152]{1,0:T(8,128)(2,1)}, u32[]{:S(2)}, u32[]{:S(2)}) collective-permute-start(bf16[64,1152]{1,0:T(8,128)(2,1)} %copy.13), channel_id=1, source_target_pairs={{0,32},{32,64},{64,96},{96,128},{128,160},{160,192},{192,224},{224... | collective-permute-start | bytes 442376 | tf_op jit(solution)/shard_map/while/body/eval_jaxpr/ppermute | solution.py:16
  246.0 8.8 %collective-permute-start.1 = (f32[64,1152]{1,0:T(8,128)}, f32[64,1152]{1,0:T(8,128)S(1)}, u32[]{:S(2)}, u32[]{:S(2)}) collective-permute-start(f32[64,1152]{1,0:T(8,128)} %fusion.80), channel_id=1, source_target_pairs={{0,32},{32,64},{64,96},{96,128},{128,160},{160,192},{192,224},{224... | collective-permute-start | bytes 884744 | tf_op jit(solution)/shard_map/while/body/eval_jaxpr/ppermute | solution.py:16
  257.2 12.4 %collective-permute-start = (bf16[64,1152]{1,0:T(8,128)(2,1)}, bf16[64,1152]{1,0:T(8,128)(2,1)}, u32[]{:S(2)}, u32[]{:S(2)}) collective-permute-start(bf16[64,1152]{1,0:T(8,128)(2,1)} %copy.13), channel_id=1, source_target_pairs={{0,32},{32,64},{64,96},{96,128},{128,160},{160,192},{192,224},{224... | collective-permute-start | bytes 442376 | tf_op jit(solution)/shard_map/while/body/eval_jaxpr/ppermute | solution.py:16
  264.7 8.8 %collective-permute-start.1 = (f32[64,1152]{1,0:T(8,128)}, f32[64,1152]{1,0:T(8,128)S(1)}, u32[]{:S(2)}, u32[]{:S(2)}) collective-permute-start(f32[64,1152]{1,0:T(8,128)} %fusion.80), channel_id=1, source_target_pairs={{0,32},{32,64},{64,96},{96,128},{128,160},{160,192},{192,224},{224... | collective-permute-start | bytes 884744 | tf_op jit(solution)/shard_map/while/body/eval_jaxpr/ppermute | solution.py:16
  275.9 12.4 %collective-permute-start = (bf16[64,1152]{1,0:T(8,128)(2,1)}, bf16[64,1152]{1,0:T(8,128)(2,1)}, u32[]{:S(2)}, u32[]{:S(2)}) collective-permute-start(bf16[64,1152]{1,0:T(8,128)(2,1)} %copy.13), channel_id=1, source_target_pairs={{0,32},{32,64},{64,96},{96,128},{128,160},{160,192},{192,224},{224... | collective-permute-start | bytes 442376 | tf_op jit(solution)/shard_map/while/body/eval_jaxpr/ppermute | solution.py:16
  283.4 8.8 %collective-permute-start.1 = (f32[64,1152]{1,0:T(8,128)}, f32[64,1152]{1,0:T(8,128)S(1)}, u32[]{:S(2)}, u32[]{:S(2)}) collective-permute-start(f32[64,1152]{1,0:T(8,128)} %fusion.80), channel_id=1, source_target_pairs={{0,32},{32,64},{64,96},{96,128},{128,160},{160,192},{192,224},{224... | collective-permute-start | bytes 884744 | tf_op jit(solution)/shard_map/while/body/eval_jaxpr/ppermute | solution.py:16
  294.6 12.4 %collective-permute-start = (bf16[64,1152]{1,0:T(8,128)(2,1)}, bf16[64,1152]{1,0:T(8,128)(2,1)}, u32[]{:S(2)}, u32[]{:S(2)}) collective-permute-start(bf16[64,1152]{1,0:T(8,128)(2,1)} %copy.13), channel_id=1, source_target_pairs={{0,32},{32,64},{64,96},{96,128},{128,160},{160,192},{192,224},{224... | collective-permute-start | bytes 442376 | tf_op jit(solution)/shard_map/while/body/eval_jaxpr/ppermute | solution.py:16
  302.2 8.8 %collective-permute-start.1 = (f32[64,1152]{1,0:T(8,128)}, f32[64,1152]{1,0:T(8,128)S(1)}, u32[]{:S(2)}, u32[]{:S(2)}) collective-permute-start(f32[64,1152]{1,0:T(8,128)} %fusion.80), channel_id=1, source_target_pairs={{0,32},{32,64},{64,96},{96,128},{128,160},{160,192},{192,224},{224... | collective-permute-start | bytes 884744 | tf_op jit(solution)/shard_map/while/body/eval_jaxpr/ppermute | solution.py:16
  313.4 12.4 %collective-permute-start = (bf16[64,1152]{1,0:T(8,128)(2,1)}, bf16[64,1152]{1,0:T(8,128)(2,1)}, u32[]{:S(2)}, u32[]{:S(2)}) collective-permute-start(bf16[64,1152]{1,0:T(8,128)(2,1)} %copy.13), channel_id=1, source_target_pairs={{0,32},{32,64},{64,96},{96,128},{128,160},{160,192},{192,224},{224... | collective-permute-start | bytes 442376 | tf_op jit(solution)/shard_map/while/body/eval_jaxpr/ppermute | solution.py:16
  320.9 8.8 %collective-permute-start.1 = (f32[64,1152]{1,0:T(8,128)}, f32[64,1152]{1,0:T(8,128)S(1)}, u32[]{:S(2)}, u32[]{:S(2)}) collective-permute-start(f32[64,1152]{1,0:T(8,128)} %fusion.80), channel_id=1, source_target_pairs={{0,32},{32,64},{64,96},{96,128},{128,160},{160,192},{192,224},{224... | collective-permute-start | bytes 884744 | tf_op jit(solution)/shard_map/while/body/eval_jaxpr/ppermute | solution.py:16
  332.1 12.4 %collective-permute-start = (bf16[64,1152]{1,0:T(8,128)(2,1)}, bf16[64,1152]{1,0:T(8,128)(2,1)}, u32[]{:S(2)}, u32[]{:S(2)}) collective-permute-start(bf16[64,1152]{1,0:T(8,128)(2,1)} %copy.13), channel_id=1, source_target_pairs={{0,32},{32,64},{64,96},{96,128},{128,160},{160,192},{192,224},{224... | collective-permute-start | bytes 442376 | tf_op jit(solution)/shard_map/while/body/eval_jaxpr/ppermute | solution.py:16
  339.6 8.8 %collective-permute-start.1 = (f32[64,1152]{1,0:T(8,128)}, f32[64,1152]{1,0:T(8,128)S(1)}, u32[]{:S(2)}, u32[]{:S(2)}) collective-permute-start(f32[64,1152]{1,0:T(8,128)} %fusion.80), channel_id=1, source_target_pairs={{0,32},{32,64},{64,96},{96,128},{128,160},{160,192},{192,224},{224... | collective-permute-start | bytes 884744 | tf_op jit(solution)/shard_map/while/body/eval_jaxpr/ppermute | solution.py:16
  350.8 12.4 %collective-permute-start = (bf16[64,1152]{1,0:T(8,128)(2,1)}, bf16[64,1152]{1,0:T(8,128)(2,1)}, u32[]{:S(2)}, u32[]{:S(2)}) collective-permute-start(bf16[64,1152]{1,0:T(8,128)(2,1)} %copy.13), channel_id=1, source_target_pairs={{0,32},{32,64},{64,96},{96,128},{128,160},{160,192},{192,224},{224... | collective-permute-start | bytes 442376 | tf_op jit(solution)/shard_map/while/body/eval_jaxpr/ppermute | solution.py:16
  358.4 8.8 %collective-permute-start.1 = (f32[64,1152]{1,0:T(8,128)}, f32[64,1152]{1,0:T(8,128)S(1)}, u32[]{:S(2)}, u32[]{:S(2)}) collective-permute-start(f32[64,1152]{1,0:T(8,128)} %fusion.80), channel_id=1, source_target_pairs={{0,32},{32,64},{64,96},{96,128},{128,160},{160,192},{192,224},{224... | collective-permute-start | bytes 884744 | tf_op jit(solution)/shard_map/while/body/eval_jaxpr/ppermute | solution.py:16
  372.5 10.3 %copy-start.4 = (bf16[64,1152]{1,0:T(8,128)(2,1)S(1)}, bf16[64,1152]{1,0:T(8,128)(2,1)}, u32[]{:S(2)}) copy-start(bf16[64,1152]{1,0:T(8,128)(2,1)} %param.9) | copy-start | bytes 442372
  372.5 10.3 %copy-start.6 = (f32[1152]{0:T(1024)S(1)}, f32[1152]{0:T(1024)}, u32[]{:S(2)}) copy-start(f32[1152]{0:T(1024)} %param.13) | copy-start | bytes 13828
  372.5 10.3 %copy-start.7 = (f32[1152]{0:T(1024)S(1)}, f32[1152]{0:T(1024)}, u32[]{:S(2)}) copy-start(f32[1152]{0:T(1024)} %param.12) | copy-start | bytes 13828
  372.5 10.3 %copy-start.13 = (f32[64]{0:T(128)S(1)}, f32[64]{0:T(128)}, u32[]{:S(2)}) copy-start(f32[64]{0:T(128)} %copy-done.12) | copy-start | bytes 772
  372.6 86.7 %copy-start.5 = (bf16[64,1152]{1,0:T(8,128)(2,1)S(1)}, bf16[64,1152]{1,0:T(8,128)(2,1)}, u32[]{:S(2)}) copy-start(bf16[64,1152]{1,0:T(8,128)(2,1)} %param.8) | copy-start | bytes 442372
  372.6 86.7 %copy-start.8 = (f32[1152]{0:T(1024)S(1)}, f32[1152]{0:T(1024)}, u32[]{:S(2)}) copy-start(f32[1152]{0:T(1024)} %param.11) | copy-start | bytes 13828
  372.6 86.7 %copy-start.9 = (f32[1152]{0:T(1024)S(1)}, f32[1152]{0:T(1024)}, u32[]{:S(2)}) copy-start(f32[1152]{0:T(1024)} %param.10) | copy-start | bytes 13828
  372.6 86.7 %copy-start.11 = (f32[64]{0:T(128)S(1)}, f32[64]{0:T(128)}, u32[]{:S(2)}) copy-start(f32[64]{0:T(128)} %copy-done.10) | copy-start | bytes 772
  374.2 8.6 %collective-permute-start.2 = (f32[64,1152]{1,0:T(8,128)S(1)}, f32[64,1152]{1,0:T(8,128)S(1)}, u32[]{:S(2)}, u32[]{:S(2)}) collective-permute-start(f32[64,1152]{1,0:T(8,128)S(1)} %fusion.12), channel_id=1, source_target_pairs={{0,32},{32,64},{64,96},{96,128},{128,160},{160,192},{192,224},{224... | collective-permute-start | bytes 884744 | tf_op jit(solution)/shard_map/ppermute | solution.py:16
  (27 other events, 80.6 us)
Sparse Core Ops, SparseCore 0:
  12.5 66.6 all-gather.1
  372.7 86.5 reduce-scatter.1
where the time goes:
time: 472 us; the launch traced here: 469 us
  waiting for transfers between devices  196 us (42%)
  starting transfers between devices  109 us (23%)
  matrix products  89.6 us (19%)
  local copies, waits for them, and re-layouts  38 us (8%)
  other arithmetic  22.5 us (5%)
  between operations  14.3 us (3%)
    ppermute x31, starting transfers between devices, from_behind(): return lax.ppermute(value, axis, pairs)  109 us
    reduce_scatter x1, waiting for transfers between devices, body(): lax.psum_scatter(image_partial, 'col', scatter_dimension=0, tiled=True)  75.1 us
    all_gather x1, waiting for transfers between devices, body(): fixed_block = lax.all_gather(own_image, 'col', axis=0, tiled=True)  61.6 us
    ppermute x31, waiting for transfers between devices, from_behind(): return lax.ppermute(value, axis, pairs)  58.8 us
    while x75, local copies, waits for them, and re-layouts  36 us
    dot_general x16, matrix products, tile_pass(): lax.dot_general(pair_grad, fixed_block, (((0,), (0,)), ((), ())), preferr...  30.3 us
    dot_general x16, matrix products, tile_pass(): lax.dot_general(fixed_block, moving, (((1,), (1,)), ((), ())), preferred_...  29.8 us
    dot_general x16, matrix products, tile_pass(): jnp.dot(pair_grad, moving, preferred_element_type=jnp.float32)  29.6 us
  transfers between devices with their start and end apart: 33, of which 18 were waited for; matrix products, arithmetic and copies ran while one was open for 21% of the time, Pallas kernels for 0%

commit v1 on v0

v1 whole, which is shorter than its diff:
```python
import jax
import jax.numpy as jnp
from jax import lax
from jax.experimental import pallas as pl
from jax.experimental.pallas import tpu as pltpu
from jax.sharding import PartitionSpec as P

logit_scale = 10.0
logit_shift = -10.0
loss_weight = 16.0
norm_eps = 1e-06
unit_eps = 1e-06
row_blocks = 4


def normalize(acts, gains, offset):
    values = acts.astype(jnp.float32)
    row_mean = jnp.mean(values, axis=-1, keepdims=True)
    centered = values - row_mean
    row_var = jnp.mean(centered * centered, axis=-1, keepdims=True)
    inverse_std = lax.rsqrt(row_var + norm_eps)
    hat_rows = centered * inverse_std
    scaled = hat_rows * gains + offset
    inverse_len = lax.rsqrt(jnp.sum(scaled * scaled, axis=-1, keepdims=True) + unit_eps)
    return (scaled * inverse_len, hat_rows, inverse_std, inverse_len)


def norm_backward(unit_grad, unit_rows, hat_rows, inverse_std, inverse_len, gains):
    along = jnp.sum(unit_rows * unit_grad, axis=-1, keepdims=True)
    grad_scaled = (unit_grad - unit_rows * along) * inverse_len
    grad_hat = grad_scaled * gains
    mean_one = jnp.mean(grad_hat, axis=-1, keepdims=True)
    mean_two = jnp.mean(grad_hat * hat_rows, axis=-1, keepdims=True)
    return inverse_std * (grad_hat - mean_one - hat_rows * mean_two)


def embed_kernel(image_ref, text_ref, ig_ref, io_ref, tg_ref, to_ref, out_ref):
    image_unit = normalize(image_ref[...], ig_ref[...], io_ref[...])[0]
    text_unit = normalize(text_ref[...], tg_ref[...], to_ref[...])[0]
    out_ref[0] = image_unit.astype(jnp.bfloat16)
    out_ref[1] = text_unit.astype(jnp.bfloat16)


def embed(image_acts, text_acts, ig, io, tg, to):
    rows, width = image_acts.shape
    return pl.pallas_call(
        embed_kernel,
        out_shape=jax.ShapeDtypeStruct((2, rows, width), jnp.bfloat16),
    )(image_acts, text_acts, ig, io, tg, to)


def pair_kernel(place_ref, fixed_ref, moving_ref, out_ref, total):
    step = pl.program_id(1)
    planes, _, group, width = moving_ref.shape
    blocks = fixed_ref.shape[0]
    fixed = fixed_ref[...].reshape(blocks * group, width)
    moving = moving_ref[...].reshape(planes * group, width)
    scores = lax.dot_general(
        fixed, moving, (((1,), (1,)), ((), ())), preferred_element_type=jnp.float32
    )
    fixed_index = lax.broadcasted_iota(jnp.int32, scores.shape, 0) - place_ref[1] * group
    moving_index = lax.broadcasted_iota(jnp.int32, scores.shape, 1)
    moving_index = moving_index + (step * planes - place_ref[0]) * group
    own = jnp.logical_and(
        fixed_index == moving_index,
        jnp.logical_and(fixed_index >= 0, fixed_index < group),
    )
    labels = jnp.where(own, jnp.float32(1.0), jnp.float32(0.0))
    pair_grad = (jax.nn.sigmoid(logit_scale * scores + logit_shift) - labels).astype(jnp.bfloat16)
    part = jnp.dot(pair_grad, moving, preferred_element_type=jnp.float32)

    @pl.when(step == 0)
    def _():
        total[...] = part

    @pl.when(step > 0)
    def _():
        total[...] += part

    @pl.when(step == pl.num_programs(1) - 1)
    def _():
        out_ref[...] = total[...].astype(jnp.bfloat16).reshape(out_ref.shape)


def pair_grads(place, fixed, moving):
    blocks, towers, group, width = fixed.shape
    planes = moving.shape[0]
    steps = row_blocks
    per_step = planes // steps
    flops = 4 * towers * blocks * planes * group * group * width
    return pl.pallas_call(
        pair_kernel,
        out_shape=jax.ShapeDtypeStruct((blocks, towers, group, width), jnp.bfloat16),
        grid_spec=pltpu.PrefetchScalarGridSpec(
            num_scalar_prefetch=1,
            grid=(towers, steps),
            in_specs=[
                pl.BlockSpec((blocks, 1, group, width), lambda t, s, place: (0, t, 0, 0)),
                pl.BlockSpec((per_step, 1, group, width), lambda t, s, place: (s, 1 - t, 0, 0)),
            ],
            out_specs=pl.BlockSpec((blocks, 1, group, width), lambda t, s, place: (0, t, 0, 0)),
            scratch_shapes=[pltpu.VMEM((blocks * group, width), jnp.float32)],
        ),
        compiler_params=pltpu.CompilerParams(vmem_limit_bytes=40 * 1024 * 1024),
        cost_estimate=pl.CostEstimate(
            flops=flops, bytes_accessed=12 * 1024 * 1024, transcendentals=1024 * 1024
        ),
    )(place, fixed, moving)


def finish_kernel(
    parts_ref, image_ref, text_ref, ig_ref, io_ref, tg_ref, to_ref, image_out, text_out
):
    parts = parts_ref[...].astype(jnp.float32)
    grads = jnp.sum(parts, axis=0) * (logit_scale * loss_weight)
    sides = (
        (grads[0], image_ref, ig_ref, io_ref, image_out),
        (grads[1], text_ref, tg_ref, to_ref, text_out),
    )
    for grad, acts_ref, gain_ref, offset_ref, out_ref in sides:
        gains = gain_ref[...]
        unit, hat, std, length = normalize(acts_ref[...], gains, offset_ref[...])
        out_ref[...] = norm_backward(grad, unit, hat, std, length, gains).astype(jnp.bfloat16)


def finish(parts, image_acts, text_acts, ig, io, tg, to):
    blocks, towers, group, width = parts.shape
    rows = 16
    acts_spec = pl.BlockSpec((rows, width), lambda i: (i, 0))
    flat_spec = pl.BlockSpec((1, width), lambda i: (0, 0))
    shape = jax.ShapeDtypeStruct((group, width), jnp.bfloat16)
    return pl.pallas_call(
        finish_kernel,
        out_shape=(shape, shape),
        grid=(group // rows,),
        in_specs=[
            pl.BlockSpec((blocks, towers, rows, width), lambda i: (0, 0, i, 0)),
            acts_spec,
            acts_spec,
            flat_spec,
            flat_spec,
            flat_spec,
            flat_spec,
        ],
        out_specs=(acts_spec, acts_spec),
    )(parts, image_acts, text_acts, ig, io, tg, to)


def body(image_acts, text_acts, image_gain, image_offset, text_gain, text_offset):
    vectors = [v[None, :] for v in (image_gain, image_offset, text_gain, text_offset)]
    own = embed(image_acts, text_acts, *vectors)
    columns = lax.axis_size("col")
    moving = lax.all_gather(own, "row", axis=0)
    copies = jnp.broadcast_to(own[None], (columns, *own.shape))
    fixed = lax.all_to_all(copies, "col", 0, 0)
    place = jnp.stack([lax.axis_index("row"), lax.axis_index("col")]).astype(jnp.int32)
    parts = pair_grads(place, fixed, moving)
    parts = lax.all_to_all(parts, "col", 0, 0)
    return finish(parts, image_acts, text_acts, *vectors)


def solution(mesh):
    placed = (P(("row", "col", "rep"), None), P(("row", "col", "rep"), None), P(), P(), P(), P())
    return jax.shard_map(
        body,
        mesh=mesh,
        in_specs=placed,
        out_specs=(P(("row", "col", "rep"), None), P(("row", "col", "rep"), None)),
        check_vma=False,
    )
```

time: 472 us -> 158 us (0.33)
  the two profiles are of different devices: /device:TPU:32 before, /device:TPU:2 now
where the time goes in v1:
time: 158 us; the launch traced here: 157 us
  waiting for transfers between devices  75.8 us (48%)
  blocking collectives  29.1 us (18%)
  Pallas kernels  22.2 us (14%)
  between operations  14 us (9%)
  local copies, waits for them, and re-layouts  10.2 us (6%)
  starting transfers between devices  6.07 us (4%)
    all_gather x1, waiting for transfers between devices, body(): moving = lax.all_gather(own, 'row', axis=0)  44.6 us
    all_to_all x1, waiting for transfers between devices, body(): fixed = lax.all_to_all(copies, 'col', 0, 0)  31.2 us
    all_to_all x1, blocking collectives, body(): parts = lax.all_to_all(parts, 'col', 0, 0)  29.1 us
    pallas_call x1, Pallas kernels, pair_grads(): pl.pallas_call(pair_kernel, out_shape=jax.ShapeDtypeStruct((blocks, tower...  15.7 us
    all_to_all x1, starting transfers between devices, body(): fixed = lax.all_to_all(copies, 'col', 0, 0)  6.03 us
    broadcast_in_dim x4, local copies, waits for them, and re-layouts, body(): v[None, :]  5.17 us
    pallas_call x1, Pallas kernels, finish(): pl.pallas_call(finish_kernel, out_shape=(shape, shape), grid=(group // ro...  4.44 us
  transfers between devices with their start and end apart: 2, of which 2 were waited for; matrix products, arithmetic and copies ran while one was open for 2% of the time, Pallas kernels for 0%

profile of v1, /device:TPU:2, one launch (start us, length us, event | category | flops | bytes accessed | tf_op | source)
XLA Modules:
  0.0 157.5 jit_solution(15009911917188430698)
XLA Ops:
  7.2 0.0 all-gather.3.cloned.1.call-start
  7.2 1.3 broadcast_in_dim.20.ig_ref
  8.5 1.3 broadcast_in_dim.21.io_ref
  9.8 1.3 broadcast_in_dim.22.tg_ref
  11.1 1.3 broadcast_in_dim.23.to_ref
  12.4 2.1 %shard_map.77 = bf16[2,64,1152]{2,1,0:T(8,128)(2,1)} custom-call(bf16[64,1152]{1,0:T(8,128)(2,1)} %image_ref.3, bf16[64,1152]{1,0:T(8,128)(2,1)} %text_ref.3, f32[1,1152]{1,0:T(1,128)} %broadcast_in_dim.20.ig_ref, f32[1,1152]{1,0:T(1,128)} %broadcast_in_dim.21.io_ref, f32[1,1152]{1,0:T(1,128)} %broadcast_in_dim.22.tg_ref, f32[1,1152]{1,0:T(1,128)} %broadcast_in_dim.23.to_ref), custom_call_target="tpu_custom_call" | custom-call | tf_op jit(solution)/shard_map/pallas_call | solution.py:46
  14.5 0.0 all-gather.3.cloned.1.call-update
  14.5 2.7 %broadcast_in_dim.24 = bf16[8,2,64,1152]{3,2,1,0:T(8,128)(2,1)} broadcast(bf16[2,64,1152]{2,1,0:T(8,128)(2,1)} %shard_map.77), dimensions={1,2,3} | broadcast | bytes 2654208 | tf_op jit(solution)/shard_map/broadcast_in_dim | solution.py:154
  17.2 6.0 %all-to-all-start = ((bf16[8,2,64,1152]{3,2,1,0:T(8,128)(2,1)}), bf16[8,2,64,1152]{3,2,1,0:T(8,128)(2,1)S(1)}, u32[]{:S(2)}, u32[]{:S(2)}) async-start(bf16[8,2,64,1152]{3,2,1,0:T(8,128)(2,1)} %broadcast_in_dim.24), calls=%async_computation | async-start | bytes 4718592 | tf_op jit(solution)/shard_map/all_to_all | solution.py:155
  23.3 0.1 pad_add_fusion.place_ref
  23.3 31.2 %all-to-all-done.fixed_ref = bf16[8,2,64,1152]{3,2,1,0:T(8,128)(2,1)S(1)} async-done(((bf16[8,2,64,1152]{3,2,1,0:T(8,128)(2,1)}), bf16[8,2,64,1152]{3,2,1,0:T(8,128)(2,1)S(1)}, u32[]{:S(2)}, u32[]{:S(2)}) %all-to-all-start) | async-done | bytes 2359328 | tf_op jit(solution)/shard_map/all_to_all | solution.py:155
  54.6 44.6 %all-gather.3.cloned.1.call-done = bf16[32,64,1152]{2,1,0:T(8,128)(2,1)} async-done(((bf16[2,64,1152]{2,1,0:T(8,128)(2,1)}), bf16[32,64,1152]{2,1,0:T(8,128)(2,1)}) %all-gather.3.cloned.1.call-update) | async-done | bytes 4718608 | tf_op jit(solution)/shard_map/all_gather | solution.py:153
  99.1 0.0 copy-start
  99.1 2.3 %copy-done = bf16[32,64,1152]{2,1,0:T(8,128)(2,1)S(1)} copy-done((bf16[32,64,1152]{2,1,0:T(8,128)(2,1)S(1)}, bf16[32,64,1152]{2,1,0:T(8,128)(2,1)}, u32[]{:S(2)}) %copy-start) | copy-done | bytes 4718616
  101.5 15.7 %shard_map.78 = bf16[8,2,64,1152]{3,2,1,0:T(8,128)(2,1)S(1)} custom-call(s32[2]{0:T(128)S(1)} %pad_add_fusion.place_ref, bf16[8,2,64,1152]{3,2,1,0:T(8,128)(2,1)S(1)} %all-to-all-done.fixed_ref, bf16[16,2,64,1152]{3,2,1,0:T(8,128)(2,1)S(1)} %bitcast.3), custom_call_target="tpu_custom_call" | custom-call | flops 4831838208 | bytes 12582912 | tf_op jit(solution)/shard_map/pallas_call | solution.py:91
  117.1 29.1 %all_to_all.10.parts_ref = bf16[8,2,64,1152]{3,2,1,0:T(8,128)(2,1)} all-to-all(bf16[8,2,64,1152]{3,2,1,0:T(8,128)(2,1)S(1)} %shard_map.78), channel_id=1, replica_groups=mesh['row'=16,'col'=8,'rep'=4] {'col'}, dimensions={0} | all-to-all | bytes 4718592 | tf_op jit(solution)/shard_map/all_to_all | solution.py:158
  146.2 4.4 %shard_map.79 = (bf16[64,1152]{1,0:T(8,128)(2,1)}, bf16[64,1152]{1,0:T(8,128)(2,1)}) custom-call(bf16[8,2,64,1152]{3,2,1,0:T(8,128)(2,1)} %all_to_all.10.parts_ref, bf16[64,1152]{1,0:T(8,128)(2,1)} %image_ref.3, bf16[64,1152]{1,0:T(8,128)(2,1)} %text_ref.3, f32[1,1152]{1,0:T(1,128)} %broadcast_in_dim.20.ig_ref, f32[1,1152]{1,0:T(1,128)} %broadcast_in_dim.21.io_ref, ...), custom_call_target="tpu_custom_call" | custom-call | tf_op jit(solution)/shard_map/pallas_call | solution.py:132
Async XLA Ops:
  7.2 92.0 %all-gather.3.cloned.1.call-start = ((), (), s32[]{:S(2)}) async-start(), calls=%async_computation.2 | async-start | bytes 5013504 | tf_op jit(solution)/shard_map/all_gather | solution.py:153
  17.2 37.3 %all-to-all-start = ((bf16[8,2,64,1152]{3,2,1,0:T(8,128)(2,1)}), bf16[8,2,64,1152]{3,2,1,0:T(8,128)(2,1)S(1)}, u32[]{:S(2)}, u32[]{:S(2)}) async-start(bf16[8,2,64,1152]{3,2,1,0:T(8,128)(2,1)} %broadcast_in_dim.24), calls=%async_computation | async-start | bytes 4718592 | tf_op jit(solution)/shard_map/all_to_all | solution.py:155
  99.1 2.3 %copy-start = (bf16[32,64,1152]{2,1,0:T(8,128)(2,1)S(1)}, bf16[32,64,1152]{2,1,0:T(8,128)(2,1)}, u32[]{:S(2)}) copy-start(bf16[32,64,1152]{2,1,0:T(8,128)(2,1)} %all-gather.3.cloned.1.call-done) | copy-start | bytes 14155780
Sparse Core Ops, SparseCore 0:
  14.6 84.4 all-gather.2

commit v2 on v0

v2 whole, which is shorter than its diff:
```python
import functools

import jax
import jax.numpy as jnp
from jax import lax
from jax.experimental import pallas as pl
from jax.experimental.pallas import tpu as pltpu
from jax.sharding import PartitionSpec as P

logit_scale = 10.0
logit_shift = -10.0
loss_weight = 16.0
norm_eps = 1e-06
unit_eps = 1e-06
log2_e = 1.4426950408889634
carry_scale = 32768.0
lanes = 128
chunk_rows = 16
block_rows = 256
ring_order = (0, 2, 4, 6, 7, 5, 3, 1)
last_last = (((1,), (1,)), ((), ()))


def split_three(value):
    first = value.astype(jnp.bfloat16)
    rest = value - first.astype(jnp.float32)
    second = rest.astype(jnp.bfloat16)
    third = (rest - second.astype(jnp.float32)).astype(jnp.bfloat16)
    return [part.astype(jnp.float32) for part in (first, second, third)]


def prepare_kernel(image_ref, text_ref, ig_ref, io_ref, tg_ref, to_ref, unit_ref, rows_ref):
    width = image_ref.shape[1]
    sides = ((image_ref, ig_ref, io_ref), (text_ref, tg_ref, to_ref))
    for tower, (acts_ref, gain_ref, offset_ref) in enumerate(sides):
        acts = acts_ref[...]
        gains = gain_ref[...].reshape(1, width)
        offset = offset_ref[...].reshape(1, width)
        values = acts.astype(jnp.float32)
        row_mean = jnp.mean(values, axis=-1, keepdims=True)
        centered = values - row_mean
        row_var = jnp.mean(centered * centered, axis=-1, keepdims=True)
        inverse_std = lax.rsqrt(row_var + norm_eps)
        hat = centered * inverse_std
        scaled = hat * gains + offset
        inverse_len = lax.rsqrt(jnp.sum(scaled * scaled, axis=-1, keepdims=True) + unit_eps)
        unit = scaled * inverse_len
        along = unit * gains
        mean_along = jnp.mean(along, axis=-1, keepdims=True)
        mean_along_hat = jnp.mean(along * hat, axis=-1, keepdims=True)
        unit_ref[tower] = (unit * carry_scale).astype(jnp.bfloat16)
        rows_ref[tower, :, :width] = acts
        lane = lax.broadcasted_iota(jnp.int32, (acts.shape[0], lanes), 1)
        record = jnp.zeros((acts.shape[0], lanes), jnp.float32)
        index = 0
        for stat in (row_mean, inverse_std, inverse_len, mean_along, mean_along_hat):
            for part in split_three(stat):
                record = jnp.where(lane == index, part, record)
                index += 1
        rows_ref[tower, :, width:] = record.astype(jnp.bfloat16)


def prepare(image_acts, text_acts, *vectors):
    rows, width = image_acts.shape
    return pl.pallas_call(
        prepare_kernel,
        out_shape=(
            jax.ShapeDtypeStruct((2, rows, width), jnp.bfloat16),
            jax.ShapeDtypeStruct((2, rows, width + lanes), jnp.bfloat16),
        ),
    )(image_acts, text_acts, *vectors)


def pair_kernel(
    place_ref,
    fixed_ref,
    ig_ref,
    io_ref,
    tg_ref,
    to_ref,
    moving_ref,
    out_ref,
    embed,
    probs,
    part,
):
    blocks, towers, group, _ = fixed_ref.shape
    columns, width = moving_ref.shape[1:]
    per_block = block_rows // group
    rate = logit_scale * log2_e / carry_scale
    shift = -logit_shift * log2_e
    vectors = ((ig_ref, io_ref), (tg_ref, to_ref))
    my_row, my_block = place_ref[0], place_ref[1]
    window = lanes // group
    pair_row = my_row // window

    def probability(scores):
        return 1.0 / (1.0 + jnp.exp2(shift - rate * scores))

    def stats_of(block, tower, start):
        record = fixed_ref[block, tower, start : start + chunk_rows, width:].astype(jnp.float32)
        return [
            record[:, 3 * k : 3 * k + 1]
            + (record[:, 3 * k + 1 : 3 * k + 2] + record[:, 3 * k + 2 : 3 * k + 3])
            for k in range(5)
        ]

    def forward(slot, tower, first):
        gains = vectors[tower][0][...].reshape(1, width)
        offset = vectors[tower][1][...].reshape(1, width)
        for index in range(per_block):
            for start in range(0, group, chunk_rows):
                mean, std, length, _, _ = stats_of(first + index, tower, start)
                acts = fixed_ref[first + index, tower, start : start + chunk_rows, :width]
                hat = (acts.astype(jnp.float32) - mean) * std
                unit = (hat * gains + offset) * length
                at = index * group + start
                embed[slot, at : at + chunk_rows] = unit.astype(jnp.bfloat16)

    def score(slot, tower):
        moving = moving_ref[1 - tower]
        fixed = embed[slot]
        scores = lax.dot_general(fixed, moving, last_last, preferred_element_type=jnp.float32)
        probs[slot] = probability(scores).astype(jnp.bfloat16)

    def label(slot, tower, first):
        mine = my_block - first

        @pl.when(jnp.logical_and(mine >= 0, mine < per_block))
        def _():
            rows = pl.ds(pl.multiple_of(mine * group, group), group)
            cols = pl.ds(pl.multiple_of(pair_row * lanes, lanes), lanes)
            scores = lax.dot_general(
                embed[slot, rows],
                moving_ref[1 - tower, cols],
                last_last,
                preferred_element_type=jnp.float32,
            )
            row_index = lax.broadcasted_iota(jnp.int32, scores.shape, 0)
            col_index = lax.broadcasted_iota(jnp.int32, scores.shape, 1)
            own = row_index == col_index - (my_row % window) * group
            value = probability(scores)
            value = jnp.where(own, value - 1.0, value)
            probs[slot, rows, cols] = value.astype(jnp.bfloat16)

    def gather_grad(slot, tower):
        part[slot] = jnp.dot(probs[slot], moving_ref[1 - tower], preferred_element_type=jnp.float32)

    def backward(slot, tower, first):
        gains = vectors[tower][0][...].reshape(1, width)
        offset = vectors[tower][1][...].reshape(1, width)
        for index in range(per_block):
            for start in range(0, group, chunk_rows):
                at = index * group + start
                mean, std, length, along_one, along_hat = stats_of(first + index, tower, start)
                acts = fixed_ref[first + index, tower, start : start + chunk_rows, :width]
                hat = (acts.astype(jnp.float32) - mean) * std
                grad = part[slot, at : at + chunk_rows]
                weighted = grad * gains
                sum_one = jnp.sum(weighted, axis=-1, keepdims=True)
                sum_hat = jnp.sum(weighted * hat, axis=-1, keepdims=True)
                sum_offset = jnp.sum(grad * offset, axis=-1, keepdims=True)
                along = length * (sum_hat + sum_offset)
                mean_one = sum_one * (1.0 / width) - along * along_one
                mean_two = sum_hat * (1.0 / width) - along * along_hat
                along = along * length
                scale = (logit_scale * loss_weight / carry_scale) * length * std
                removed = (hat * gains + offset) * (gains * along) + hat * mean_two + mean_one
                value = (weighted - removed) * scale
                place = ring_order[first + index]
                out_ref[place, tower, start : start + chunk_rows] = value.astype(jnp.bfloat16)

    jobs = [(t, b) for t in range(towers) for b in range(0, blocks, per_block)]
    for slot, (tower, first) in enumerate(jobs):
        forward(slot, tower, first)
        score(slot, tower)
    for slot, (tower, first) in enumerate(jobs):
        label(slot, tower, first)
    for slot, (tower, first) in enumerate(jobs):
        gather_grad(slot, tower)
        backward(slot, tower, first)


def pair_grads(place, fixed, vectors, moving):
    blocks, towers, group, _ = fixed.shape
    columns, width = moving.shape[1:]
    slots = towers * blocks * group // block_rows
    whole = pl.BlockSpec(memory_space=pltpu.VMEM)
    return pl.pallas_call(
        pair_kernel,
        out_shape=jax.ShapeDtypeStruct((blocks, towers, group, width), jnp.bfloat16),
        in_specs=[pl.BlockSpec(memory_space=pltpu.SMEM)] + [whole] * 6,
        out_specs=whole,
        scratch_shapes=[
            pltpu.VMEM((slots, block_rows, width), jnp.bfloat16),
            pltpu.VMEM((slots, block_rows, columns), jnp.bfloat16),
            pltpu.VMEM((slots, block_rows, width), jnp.float32),
        ],
        compiler_params=pltpu.CompilerParams(vmem_limit_bytes=32 * 1024 * 1024),
        cost_estimate=pl.CostEstimate(
            flops=4 * towers * blocks * group * columns * width,
            bytes_accessed=12 * 1024 * 1024,
            transcendentals=2 * towers * blocks * group * columns,
        ),
    )(place, fixed, *vectors, moving)


def add_kernel(parts_ref, image_ref, text_ref):
    for tower, out_ref in enumerate((image_ref, text_ref)):
        total = parts_ref[0, tower].astype(jnp.float32)
        for block in range(1, parts_ref.shape[0]):
            total = total + parts_ref[block, tower].astype(jnp.float32)
        out_ref[...] = total.astype(jnp.bfloat16)


def add_parts(parts):
    _, _, group, width = parts.shape
    shape = jax.ShapeDtypeStruct((group, width), jnp.bfloat16)
    return pl.pallas_call(add_kernel, out_shape=(shape, shape))(parts)


def body(image_acts, text_acts, image_gain, image_offset, text_gain, text_offset):
    vectors = (image_gain, image_offset, text_gain, text_offset)
    units, rows = prepare(image_acts, text_acts, *vectors)
    fixed = lax.all_gather(rows, "col", axis=0, axis_index_groups=[list(ring_order)])
    moving = lax.all_gather(units.astype(jnp.float16), "row", axis=0)
    moving = jnp.swapaxes(moving, 0, 1).astype(jnp.bfloat16)
    moving = moving.reshape(moving.shape[0], -1, moving.shape[-1])
    col = lax.axis_index("col")
    my_block = jnp.where(col % 2 == 0, col // 2, 7 - col // 2)
    place = jnp.stack([lax.axis_index("row"), my_block]).astype(jnp.int32)
    parts = pair_grads(place, fixed, vectors, moving)
    parts = lax.all_to_all(parts, "col", 0, 0)
    return add_parts(parts)


def solution(mesh):
    placed = (P(("row", "col", "rep"), None), P(("row", "col", "rep"), None), P(), P(), P(), P())
    return jax.shard_map(
        body,
        mesh=mesh,
        in_specs=placed,
        out_specs=(P(("row", "col", "rep"), None), P(("row", "col", "rep"), None)),
        check_vma=False,
    )
```

time: 472 us -> 148 us (0.31)
  the two profiles are of different devices: /device:TPU:32 before, /device:TPU:2 now
where the time goes in v2:
time: 148 us
  blocking collectives  104 us (70%)
  Pallas kernels  21.4 us (14%)
  between operations  14.1 us (10%)
  local copies, waits for them, and re-layouts  6.63 us (4%)
  other arithmetic  2.15 us (1%)
    all_gather x1, blocking collectives, body(): moving = lax.all_gather(units.astype(jnp.float16), 'row', axis=0)  68.4 us
    all_to_all x1, blocking collectives, body(): parts = lax.all_to_all(parts, 'col', 0, 0)  35.4 us
    pallas_call x1, Pallas kernels, pair_grads(): pl.pallas_call(pair_kernel, out_shape=jax.ShapeDtypeStruct((blocks, tower...  16.4 us
    unnamed x12, local copies, waits for them, and re-layouts  4.09 us
  transfers between devices with their start and end apart: 1, of which 0 were waited for; matrix products, arithmetic and copies ran while one was open for 3% of the time, Pallas kernels for 0%

profile of v2, /device:TPU:2, one launch (start us, length us, event | category | flops | bytes accessed | tf_op | source)
XLA Modules:
  0.0 148.1 jit_solution(6702107480666745329)
XLA Ops:
  7.2 0.0 all-gather.5.cloned.1.call-start
  7.2 2.3 %shard_map.77 = (bf16[2,64,1152]{2,1,0:T(8,128)(2,1)}, bf16[2,64,1280]{2,1,0:T(8,128)(2,1)}) custom-call(bf16[64,1152]{1,0:T(8,128)(2,1)} %image_ref.1, bf16[64,1152]{1,0:T(8,128)(2,1)} %text_ref.1, f32[1152]{0:T(1024)} %ig_ref.3, f32[1152]{0:T(1024)} %io_ref.3, f32[1152]{0:T(1024)} %tg_ref.3, f32[1152]{0:T(1024)} %to_ref.3), custom_call_target="tpu_custom_call" | custom-call | tf_op jit(solution)/shard_map/pallas_call | solution.py:65
  9.5 0.0 all-gather.5.cloned.1.call-update
  9.5 1.0 convert_element_type.9
  10.6 68.4 %all-gather.6 = f16[32,64,1152]{2,1,0:T(8,128)(2,1)S(1)} all-gather(f16[2,64,1152]{2,1,0:T(8,128)(2,1)S(1)} %convert_element_type.9), channel_id=3, replica_groups=mesh['row'=16,'col'=8,'rep'=4] {'row'}, dimensions={0}, use_global_device_ids=true | all-gather | bytes 5013504 | tf_op jit(solution)/shard_map/all_gather | solution.py:226
  79.0 1.1 convert_element_type.12
  80.1 0.0 copy-start.1
  80.1 0.0 copy-start.2
  80.1 0.0 copy-start.3
  80.1 0.0 copy-start.4
  80.1 2.5 %copy.9 = bf16[16,2,64,1152]{3,2,0,1:T(8,128)(2,1)} copy(bf16[16,2,64,1152]{3,2,1,0:T(8,128)(2,1)S(1)} %bitcast.9) | data formatting | bytes 9437184 | tf_op jit(solution)/shard_map/convert_element_type | solution.py:227
  82.7 0.1 pad_add_fusion.place_ref
  82.7 0.0 all-gather.5.cloned.1.call-done
  82.7 0.0 copy-done.1
  82.7 0.0 copy-done.2
  82.7 0.0 copy-done.3
  82.7 0.0 copy-done.4
  82.7 0.0 copy-start
  82.8 2.3 %copy-done = bf16[16,2,64,1152]{3,2,0,1:T(8,128)(2,1)S(1)} copy-done((bf16[16,2,64,1152]{3,2,0,1:T(8,128)(2,1)S(1)}, bf16[16,2,64,1152]{3,2,0,1:T(8,128)(2,1)}, u32[]{:S(2)}) %copy-start) | copy-done | bytes 4718616
  85.1 0.0 copy-start.5
  85.1 1.7 %copy-done.5 = bf16[16,64,1280]{2,1,0:T(8,128)(2,1)S(1)} copy-done((bf16[16,64,1280]{2,1,0:T(8,128)(2,1)S(1)}, bf16[16,64,1280]{2,1,0:T(8,128)(2,1)}, u32[]{:S(2)}) %copy-start.5) | copy-done | bytes 2621464
  86.8 16.4 %shard_map.78 = bf16[8,2,64,1152]{3,2,1,0:T(8,128)(2,1)S(1)} custom-call(s32[2]{0:T(128)S(1)} %pad_add_fusion.place_ref, bf16[8,2,64,1280]{3,2,1,0:T(8,128)(2,1)S(1)} %bitcast.8, f32[1152]{0:T(1024)S(1)} %copy-done.1, f32[1152]{0:T(1024)S(1)} %copy-done.2, f32[1152]{0:T(1024)S(1)} %copy-done.3, f32[1152]{0:T(1024)S(1)} %copy-done.4, ...), custom_call_target="tpu_custom_call" | custom-call | flops 4831838208 | bytes 12582912 | tf_op jit(solution)/shard_map/pallas_call | solution.py:189
  103.3 35.4 %all_to_all.5.parts_ref = bf16[8,2,64,1152]{3,2,1,0:T(8,128)(2,1)} all-to-all(bf16[8,2,64,1152]{3,2,1,0:T(8,128)(2,1)S(1)} %shard_map.78), channel_id=1, replica_groups=mesh['row'=16,'col'=8,'rep'=4] {'col'}, dimensions={0} | all-to-all | bytes 4718592 | tf_op jit(solution)/shard_map/all_to_all | solution.py:233
  138.6 2.6 %shard_map.79 = (bf16[64,1152]{1,0:T(8,128)(2,1)}, bf16[64,1152]{1,0:T(8,128)(2,1)}) custom-call(bf16[8,2,64,1152]{3,2,1,0:T(8,128)(2,1)} %all_to_all.5.parts_ref), custom_call_target="tpu_custom_call" | custom-call | tf_op jit(solution)/shard_map/pallas_call | solution.py:219
Async XLA Ops:
  7.2 75.6 %all-gather.5.cloned.1.call-start = ((), (), s32[]{:S(2)}) async-start(), calls=%async_computation.1 | async-start | bytes 2949120 | tf_op jit(solution)/shard_map/all_gather | solution.py:225
  80.1 2.7 %copy-start.1 = (f32[1152]{0:T(1024)S(1)}, f32[1152]{0:T(1024)}, u32[]{:S(2)}) copy-start(f32[1152]{0:T(1024)} %ig_ref.3) | copy-start | bytes 13828
  80.1 2.7 %copy-start.2 = (f32[1152]{0:T(1024)S(1)}, f32[1152]{0:T(1024)}, u32[]{:S(2)}) copy-start(f32[1152]{0:T(1024)} %io_ref.3) | copy-start | bytes 13828
  80.1 2.6 %copy-start.3 = (f32[1152]{0:T(1024)S(1)}, f32[1152]{0:T(1024)}, u32[]{:S(2)}) copy-start(f32[1152]{0:T(1024)} %tg_ref.3) | copy-start | bytes 13828
  80.1 2.6 %copy-start.4 = (f32[1152]{0:T(1024)S(1)}, f32[1152]{0:T(1024)}, u32[]{:S(2)}) copy-start(f32[1152]{0:T(1024)} %to_ref.3) | copy-start | bytes 13828
  82.7 2.3 %copy-start = (bf16[16,2,64,1152]{3,2,0,1:T(8,128)(2,1)S(1)}, bf16[16,2,64,1152]{3,2,0,1:T(8,128)(2,1)}, u32[]{:S(2)}) copy-start(bf16[16,2,64,1152]{3,2,0,1:T(8,128)(2,1)} %copy.9) | copy-start | bytes 14155780
  85.1 1.7 %copy-start.5 = (bf16[16,64,1280]{2,1,0:T(8,128)(2,1)S(1)}, bf16[16,64,1280]{2,1,0:T(8,128)(2,1)}, u32[]{:S(2)}) copy-start(bf16[16,64,1280]{2,1,0:T(8,128)(2,1)} %all-gather.5.cloned.1.call-done) | copy-start | bytes 7864324
Sparse Core Ops, SparseCore 0:
  10.1 51.2 all-gather.4

commit v3 on v2

v3 whole, which is shorter than its diff:
```python
import functools

import jax
import jax.numpy as jnp
from jax import lax
from jax.experimental import pallas as pl
from jax.experimental.pallas import tpu as pltpu
from jax.sharding import PartitionSpec as P

logit_scale = 10.0
logit_shift = -10.0
loss_weight = 16.0
norm_eps = 1e-06
unit_eps = 1e-06
log2_e = 1.4426950408889634
carry_scale = 32768.0
lanes = 128
chunk_rows = 16
block_rows = 256
stat_count = 5
ring_order = (0, 1, 2, 3, 4, 5, 6, 7)
last_last = (((1,), (1,)), ((), ()))


def split_three(value):
    first = value.astype(jnp.bfloat16)
    rest = value - first.astype(jnp.float32)
    second = rest.astype(jnp.bfloat16)
    third = (rest - second.astype(jnp.float32)).astype(jnp.bfloat16)
    return [part.astype(jnp.float32) for part in (first, second, third)]


def prepare_kernel(image_ref, text_ref, ig_ref, io_ref, tg_ref, to_ref, unit_ref, rows_ref):
    width = image_ref.shape[1]
    sides = ((image_ref, ig_ref, io_ref), (text_ref, tg_ref, to_ref))
    for tower, (acts_ref, gain_ref, offset_ref) in enumerate(sides):
        acts = acts_ref[...]
        gains = gain_ref[...].reshape(1, width)
        offset = offset_ref[...].reshape(1, width)
        values = acts.astype(jnp.float32)
        row_mean = jnp.mean(values, axis=-1, keepdims=True)
        centered = values - row_mean
        row_var = jnp.mean(centered * centered, axis=-1, keepdims=True)
        inverse_std = lax.rsqrt(row_var + norm_eps)
        hat = centered * inverse_std
        scaled = hat * gains + offset
        inverse_len = lax.rsqrt(jnp.sum(scaled * scaled, axis=-1, keepdims=True) + unit_eps)
        unit = scaled * inverse_len
        along = unit * gains
        mean_along = jnp.mean(along, axis=-1, keepdims=True)
        mean_along_hat = jnp.mean(along * hat, axis=-1, keepdims=True)
        unit_ref[tower] = (unit * carry_scale).astype(jnp.bfloat16)
        for copy in range(rows_ref.shape[0]):
            rows_ref[copy, tower, :, :width] = acts
        lane = lax.broadcasted_iota(jnp.int32, (acts.shape[0], lanes), 1)
        record = jnp.zeros((acts.shape[0], lanes), jnp.float32)
        index = 0
        for stat in (row_mean, inverse_std, inverse_len, mean_along, mean_along_hat):
            for part in split_three(stat):
                record = jnp.where(lane == index, part, record)
                index += 1
        record = record.astype(jnp.bfloat16)
        for copy in range(rows_ref.shape[0]):
            rows_ref[copy, tower, :, width:] = record


def prepare(copies, image_acts, text_acts, *vectors):
    rows, width = image_acts.shape
    return pl.pallas_call(
        prepare_kernel,
        out_shape=(
            jax.ShapeDtypeStruct((2, rows, width), jnp.bfloat16),
            jax.ShapeDtypeStruct((copies, 2, rows, width + lanes), jnp.bfloat16),
        ),
    )(image_acts, text_acts, *vectors)


def pair_kernel(
    place_ref,
    fixed_ref,
    ig_ref,
    io_ref,
    tg_ref,
    to_ref,
    moving_hbm,
    out_ref,
    moving_ref,
    arrived,
    stats,
    embed,
    probs,
    part,
):
    blocks, towers, group, _ = fixed_ref.shape
    _, planes, _, width = moving_ref.shape
    columns = planes * group
    per_block = block_rows // group
    rate = logit_scale * log2_e / carry_scale
    shift = -logit_shift * log2_e
    copies = [
        pltpu.make_async_copy(moving_hbm.at[:, t], moving_ref.at[t], arrived.at[t])
        for t in range(towers)
    ]
    for copy in reversed(copies):
        copy.start()
    vectors = ((ig_ref, io_ref), (tg_ref, to_ref))
    my_row, my_block = place_ref[0], place_ref[1]
    window = lanes // group
    pair_row = my_row // window
    spread_rows = lax.broadcasted_iota(jnp.int32, (lanes, stat_count * lanes), 0)
    spread_cols = lax.broadcasted_iota(jnp.int32, (lanes, stat_count * lanes), 1)
    spread = spread_rows // 3 == spread_cols // lanes
    spread = jnp.where(spread, jnp.float32(1.0), jnp.float32(0.0)).astype(jnp.bfloat16)

    def probability(scores):
        return 1.0 / (1.0 + jnp.exp2(shift - rate * scores))

    def moving_rows(tower):
        return moving_ref[1 - tower].reshape(columns, width)

    def wide(value):
        return jnp.concatenate([value] * (width // lanes), axis=1)

    def chunks(first):
        for index in range(per_block):
            for start in range(0, group, chunk_rows):
                yield first + index, start, index * group + start

    def stat(slot, at, which):
        return stats[slot, at : at + chunk_rows, which * lanes : (which + 1) * lanes]

    def hat_rows(slot, tower, block, start, at):
        acts = fixed_ref[block, tower, start : start + chunk_rows, :width].astype(jnp.float32)
        return (acts - wide(stat(slot, at, 0))) * wide(stat(slot, at, 1))

    def forward(slot, tower, first):
        gains = vectors[tower][0][...].reshape(1, width)
        offset = vectors[tower][1][...].reshape(1, width)
        record = fixed_ref[first : first + per_block, tower, :, width:].reshape(block_rows, lanes)
        stats[slot] = jnp.dot(record, spread, preferred_element_type=jnp.float32)
        for block, start, at in chunks(first):
            hat = hat_rows(slot, tower, block, start, at)
            unit = (hat * gains + offset) * wide(stat(slot, at, 2))
            embed[slot, at : at + chunk_rows] = unit.astype(jnp.bfloat16)

    def score(slot, tower):
        scores = lax.dot_general(
            embed[slot], moving_rows(tower), last_last, preferred_element_type=jnp.float32
        )
        probs[slot] = probability(scores).astype(jnp.bfloat16)

    def label(tower):
        slot = tower * (blocks // per_block) + my_block // per_block
        start = (my_block % per_block) * group
        rows = pl.ds(pl.multiple_of(start, group), group)
        cols = pl.ds(pl.multiple_of(pair_row * lanes, lanes), lanes)
        near = moving_ref[1 - tower, pl.ds(pair_row * window, window)].reshape(lanes, width)
        scores = lax.dot_general(
            embed[slot, rows], near, last_last, preferred_element_type=jnp.float32
        )
        row_index = lax.broadcasted_iota(jnp.int32, scores.shape, 0)
        col_index = lax.broadcasted_iota(jnp.int32, scores.shape, 1)
        own = row_index == col_index - (my_row % window) * group
        value = probability(scores)
        value = jnp.where(own, value - 1.0, value)
        probs[slot, rows, cols] = value.astype(jnp.bfloat16)

    def collect(slot, tower):
        part[slot] = jnp.dot(probs[slot], moving_rows(tower), preferred_element_type=jnp.float32)

    def backward(slot, tower, first):
        gains = vectors[tower][0][...].reshape(1, width)
        offset = vectors[tower][1][...].reshape(1, width)
        gains_two = gains * gains
        gains_offset = gains * offset
        for block, start, at in chunks(first):
            hat = hat_rows(slot, tower, block, start, at)
            grad = part[slot, at : at + chunk_rows]
            weighted = grad * gains
            sum_one = jnp.sum(weighted, axis=-1, keepdims=True)
            sum_hat = jnp.sum(weighted * hat, axis=-1, keepdims=True)
            sum_offset = jnp.sum(grad * offset, axis=-1, keepdims=True)
            length = stat(slot, at, 2)
            along = length * (sum_hat + sum_offset)
            mean_one = sum_one * (1.0 / width) - along * stat(slot, at, 3)
            mean_two = sum_hat * (1.0 / width) - along * stat(slot, at, 4)
            along = wide(along * length)
            scale = (logit_scale * loss_weight / carry_scale) * length * stat(slot, at, 1)
            removed = hat * (gains_two * along + wide(mean_two))
            removed = removed + (gains_offset * along + wide(mean_one))
            value = (weighted - removed) * wide(scale)
            out_ref[ring_order[block], tower, start : start + chunk_rows] = value.astype(
                jnp.bfloat16
            )

    jobs = [(t, b) for t in range(towers) for b in range(0, blocks, per_block)]
    for slot, (tower, first) in enumerate(jobs):
        forward(slot, tower, first)
    for slot, (tower, first) in enumerate(jobs):
        if first == 0:
            copies[1 - tower].wait()
        score(slot, tower)
    for tower in range(towers):
        label(tower)
    for slot, (tower, first) in enumerate(jobs):
        collect(slot, tower)
        backward(slot, tower, first)


def pair_grads(place, fixed, vectors, moving):
    blocks, towers, group, _ = fixed.shape
    planes, _, _, width = moving.shape
    columns = planes * group
    slots = towers * blocks * group // block_rows
    whole = pl.BlockSpec(memory_space=pltpu.VMEM)
    return pl.pallas_call(
        pair_kernel,
        out_shape=jax.ShapeDtypeStruct((blocks, towers, group, width), jnp.bfloat16),
        in_specs=[pl.BlockSpec(memory_space=pltpu.SMEM)]
        + [whole] * 5
        + [pl.BlockSpec(memory_space=pl.ANY)],
        out_specs=whole,
        scratch_shapes=[
            pltpu.VMEM((towers, planes, group, width), jnp.bfloat16),
            pltpu.SemaphoreType.DMA((towers,)),
            pltpu.VMEM((slots, block_rows, stat_count * lanes), jnp.float32),
            pltpu.VMEM((slots, block_rows, width), jnp.bfloat16),
            pltpu.VMEM((slots, block_rows, columns), jnp.bfloat16),
            pltpu.VMEM((slots, block_rows, width), jnp.float32),
        ],
        compiler_params=pltpu.CompilerParams(vmem_limit_bytes=24 * 1024 * 1024),
        cost_estimate=pl.CostEstimate(
            flops=4 * towers * blocks * group * columns * width,
            bytes_accessed=12 * 1024 * 1024,
            transcendentals=2 * towers * blocks * group * columns,
        ),
    )(place, fixed, *vectors, moving)


def add_kernel(parts_ref, image_ref, text_ref):
    for tower, out_ref in enumerate((image_ref, text_ref)):
        total = parts_ref[0, tower].astype(jnp.float32)
        for block in range(1, parts_ref.shape[0]):
            total = total + parts_ref[block, tower].astype(jnp.float32)
        out_ref[...] = total.astype(jnp.bfloat16)


def add_parts(parts):
    _, _, group, width = parts.shape
    shape = jax.ShapeDtypeStruct((group, width), jnp.bfloat16)
    return pl.pallas_call(add_kernel, out_shape=(shape, shape))(parts)


def body(image_acts, text_acts, image_gain, image_offset, text_gain, text_offset):
    vectors = (image_gain, image_offset, text_gain, text_offset)
    units, copies = prepare(lax.axis_size("col"), image_acts, text_acts, *vectors)
    fixed = lax.all_to_all(copies, "col", 0, 0)
    moving = lax.all_gather(units.astype(jnp.float16), "row", axis=0)
    moving = moving.astype(jnp.bfloat16)
    col = lax.axis_index("col")
    my_block = col
    place = jnp.stack([lax.axis_index("row"), my_block]).astype(jnp.int32)
    moving = pltpu.with_memory_space_constraint(moving, pltpu.HBM)
    parts = pair_grads(place, fixed, vectors, moving)
    parts = lax.all_to_all(parts, "col", 0, 0)
    grads = []
    for tower in range(parts.shape[1]):
        total = parts[0, tower].astype(jnp.float32)
        for block in range(1, parts.shape[0]):
            total = total + parts[block, tower].astype(jnp.float32)
        grads.append(total.astype(jnp.bfloat16))
    return tuple(grads)


def solution(mesh):
    placed = (P(("row", "col", "rep"), None), P(("row", "col", "rep"), None), P(), P(), P(), P())
    return jax.shard_map(
        body,
        mesh=mesh,
        in_specs=placed,
        out_specs=(P(("row", "col", "rep"), None), P(("row", "col", "rep"), None)),
        check_vma=False,
    )
```

time: 148 us -> 128 us (0.86)
  between operations: 14.1 us -> 0.68 us
  Pallas kernels: 21.4 us -> 13.2 us
  local copies, waits for them, and re-layouts: 6.63 us -> 0.02 us
  starting transfers between devices: 0.04 us -> 6.16 us
  other arithmetic: 2.15 us -> 4.32 us
    pallas_call x1, Pallas kernels: 16.4 us -> 9.99 us  [pair_grads(): pl.pallas_call(pair_kernel, out_shape=jax.ShapeDtypeStruct((blocks, tower...]
    all_to_all x0 -> x1, starting transfers between devices: none -> 6.16 us  [body(): fixed = lax.all_to_all(copies, 'col', 0, 0)]
    unnamed x12 -> x10, local copies, waits for them, and re-layouts: 4.09 us -> 0.02 us
    convert_element_type x1 -> x2, other arithmetic: 1.06 us -> 4.2 us  [the longest x1 3.18 us: body(): moving = moving.astype(jnp.bfloat16)]
    pallas_call x1 -> x0, Pallas kernels: 2.63 us -> none  [add_parts(): return pl.pallas_call(add_kernel, out_shape=(shape, shape))(parts)]
    convert_element_type x1 -> x0, local copies, waits for them, and re-layouts: 2.53 us -> none  [body(): moving = jnp.swapaxes(moving, 0, 1).astype(jnp.bfloat16)]
    all_to_all x1, blocking collectives: 35.4 us -> 33.2 us  [body(): parts = lax.all_to_all(parts, 'col', 0, 0)]
    all_gather x1, blocking collectives: 68.4 us -> 70.4 us  [body(): moving = lax.all_gather(units.astype(jnp.float16), 'row', axis=0)]
where the time goes in v3:
time: 128 us
  blocking collectives  104 us (81%)
  Pallas kernels  13.2 us (10%)
  starting transfers between devices  6.16 us (5%)
  other arithmetic  4.32 us (3%)
    all_gather x1, blocking collectives, body(): moving = lax.all_gather(units.astype(jnp.float16), 'row', axis=0)  70.4 us
    all_to_all x1, blocking collectives, body(): parts = lax.all_to_all(parts, 'col', 0, 0)  33.2 us
    pallas_call x1, Pallas kernels, pair_grads(): pl.pallas_call(pair_kernel, out_shape=jax.ShapeDtypeStruct((blocks, tower...  9.99 us
    all_to_all x1, starting transfers between devices, body(): fixed = lax.all_to_all(copies, 'col', 0, 0)  6.16 us
    pallas_call x1, Pallas kernels, prepare(): pl.pallas_call(prepare_kernel, out_shape=(jax.ShapeDtypeStruct((2, rows,...  3.25 us
    convert_element_type x1, other arithmetic, body(): moving = moving.astype(jnp.bfloat16)  3.18 us
  transfers between devices with their start and end apart: 1, of which 0 were waited for; matrix products, arithmetic and copies ran while one was open for 3% of the time, Pallas kernels for 0%

profile of v3, /device:TPU:2, one launch (start us, length us, event | category | flops | bytes accessed | tf_op | source)
XLA Modules:
  0.0 128.1 jit_solution(2416228141644874564)
XLA Ops:
  0.6 3.3 %shard_map.77 = (bf16[2,64,1152]{2,1,0:T(8,128)(2,1)}, bf16[8,2,64,1280]{3,2,1,0:T(8,128)(2,1)}) custom-call(bf16[64,1152]{1,0:T(8,128)(2,1)} %image_ref.1, bf16[64,1152]{1,0:T(8,128)(2,1)} %text_ref.1, f32[1152]{0:T(1024)} %ig_ref.3, f32[1152]{0:T(1024)} %io_ref.3, f32[1152]{0:T(1024)} %tg_ref.3, f32[1152]{0:T(1024)} %to_ref.3), custom_call_target="tpu_custom_call" | custom-call | tf_op jit(solution)/shard_map/pallas_call | solution.py:69
  3.9 0.0 copy-start.4
  3.9 6.2 %all-to-all-start = ((bf16[8,2,64,1280]{3,2,1,0:T(8,128)(2,1)}), bf16[8,2,64,1280]{3,2,1,0:T(8,128)(2,1)S(1)}, u32[]{:S(2)}, u32[]{:S(2)}) async-start(bf16[8,2,64,1280]{3,2,1,0:T(8,128)(2,1)} %get-tuple-element.4), calls=%async_computation | async-start | bytes 5242880 | tf_op jit(solution)/shard_map/all_to_all | solution.py:257
  10.0 0.0 copy-done.4
  10.1 0.1 convert_element_type.92
  10.1 70.4 %all-gather.2 = f16[32,64,1152]{2,1,0:T(8,128)(2,1)S(1)} all-gather(f16[2,64,1152]{2,1,0:T(8,128)(2,1)S(1)} %convert_element_type.92), channel_id=2, replica_groups=mesh['row'=16,'col'=8,'rep'=4] {'row'}, dimensions={0}, use_global_device_ids=true | all-gather | bytes 5013504 | tf_op jit(solution)/shard_map/all_gather | solution.py:258
  80.6 0.0 copy-start
  80.6 0.0 copy-start.1
  80.6 0.0 copy-start.2
  80.6 0.0 copy-start.3
  80.6 3.2 %convert_element_type.128 = bf16[32,64,1152]{2,1,0:T(8,128)(2,1)} convert(f16[32,64,1152]{2,1,0:T(8,128)(2,1)S(1)} %all-gather.2) | non-fusion elementwise | flops 2359296 | bytes 9437184 | tf_op jit(solution)/shard_map/convert_element_type | solution.py:259
  83.7 0.1 pad_add_fusion.place_ref
  83.8 0.0 all-to-all-done.fixed_ref
  83.8 0.0 copy-done
  83.8 0.0 copy-done.1
  83.8 0.0 copy-done.2
  83.8 0.0 copy-done.3
  83.9 10.0 %shard_map.78 = bf16[8,2,64,1152]{3,2,1,0:T(8,128)(2,1)S(1)} custom-call(s32[2]{0:T(128)S(1)} %pad_add_fusion.place_ref, bf16[8,2,64,1280]{3,2,1,0:T(8,128)(2,1)S(1)} %all-to-all-done.fixed_ref, f32[1152]{0:T(1024)S(1)} %copy-done, f32[1152]{0:T(1024)S(1)} %copy-done.1, f32[1152]{0:T(1024)S(1)} %copy-done.2, f32[1152]{0:T(1024)S(1)} %copy-done.3, ...), custom_call_target="tpu_custom_call" | custom-call | flops 4831838208 | bytes 12582912 | tf_op jit(solution)/shard_map/pallas_call | solution.py:216
  93.9 33.2 %all_to_all.10 = bf16[8,2,64,1152]{3,2,1,0:T(8,128)(2,1)S(1)} all-to-all(bf16[8,2,64,1152]{3,2,1,0:T(8,128)(2,1)S(1)} %shard_map.78), channel_id=1, replica_groups=mesh['row'=16,'col'=8,'rep'=4] {'col'}, dimensions={0} | all-to-all | bytes 4718592 | tf_op jit(solution)/shard_map/all_to_all | solution.py:265
  127.1 1.0 fusion.1
Async XLA Ops:
  3.9 6.2 %copy-start.4 = (bf16[2,64,1152]{2,1,0:T(8,128)(2,1)S(1)}, bf16[2,64,1152]{2,1,0:T(8,128)(2,1)}, u32[]{:S(2)}) copy-start(bf16[2,64,1152]{2,1,0:T(8,128)(2,1)} %get-tuple-element.5) | copy-start | bytes 884740
  3.9 79.9 %all-to-all-start = ((bf16[8,2,64,1280]{3,2,1,0:T(8,128)(2,1)}), bf16[8,2,64,1280]{3,2,1,0:T(8,128)(2,1)S(1)}, u32[]{:S(2)}, u32[]{:S(2)}) async-start(bf16[8,2,64,1280]{3,2,1,0:T(8,128)(2,1)} %get-tuple-element.4), calls=%async_computation | async-start | bytes 5242880 | tf_op jit(solution)/shard_map/all_to_all | solution.py:257
  80.6 3.3 %copy-start = (f32[1152]{0:T(1024)S(1)}, f32[1152]{0:T(1024)}, u32[]{:S(2)}) copy-start(f32[1152]{0:T(1024)} %ig_ref.3) | copy-start | bytes 13828
  80.6 3.3 %copy-start.1 = (f32[1152]{0:T(1024)S(1)}, f32[1152]{0:T(1024)}, u32[]{:S(2)}) copy-start(f32[1152]{0:T(1024)} %io_ref.3) | copy-start | bytes 13828
  80.6 3.3 %copy-start.2 = (f32[1152]{0:T(1024)S(1)}, f32[1152]{0:T(1024)}, u32[]{:S(2)}) copy-start(f32[1152]{0:T(1024)} %tg_ref.3) | copy-start | bytes 13828
  80.6 3.3 %copy-start.3 = (f32[1152]{0:T(1024)S(1)}, f32[1152]{0:T(1024)}, u32[]{:S(2)}) copy-start(f32[1152]{0:T(1024)} %to_ref.3) | copy-start | bytes 13828

commit v4 on v3

--- a/solution.py
+++ b/solution.py
@@ -32,45 +32,51 @@
 
 def prepare_kernel(image_ref, text_ref, ig_ref, io_ref, tg_ref, to_ref, unit_ref, rows_ref):
     width = image_ref.shape[1]
-    sides = ((image_ref, ig_ref, io_ref), (text_ref, tg_ref, to_ref))
-    for tower, (acts_ref, gain_ref, offset_ref) in enumerate(sides):
-        acts = acts_ref[...]
-        gains = gain_ref[...].reshape(1, width)
-        offset = offset_ref[...].reshape(1, width)
-        values = acts.astype(jnp.float32)
-        row_mean = jnp.mean(values, axis=-1, keepdims=True)
-        centered = values - row_mean
-        row_var = jnp.mean(centered * centered, axis=-1, keepdims=True)
-        inverse_std = lax.rsqrt(row_var + norm_eps)
-        hat = centered * inverse_std
-        scaled = hat * gains + offset
-        inverse_len = lax.rsqrt(jnp.sum(scaled * scaled, axis=-1, keepdims=True) + unit_eps)
-        unit = scaled * inverse_len
-        along = unit * gains
-        mean_along = jnp.mean(along, axis=-1, keepdims=True)
-        mean_along_hat = jnp.mean(along * hat, axis=-1, keepdims=True)
-        unit_ref[tower] = (unit * carry_scale).astype(jnp.bfloat16)
-        for copy in range(rows_ref.shape[0]):
-            rows_ref[copy, tower, :, :width] = acts
-        lane = lax.broadcasted_iota(jnp.int32, (acts.shape[0], lanes), 1)
-        record = jnp.zeros((acts.shape[0], lanes), jnp.float32)
-        index = 0
-        for stat in (row_mean, inverse_std, inverse_len, mean_along, mean_along_hat):
-            for part in split_three(stat):
-                record = jnp.where(lane == index, part, record)
-                index += 1
-        record = record.astype(jnp.bfloat16)
-        for copy in range(rows_ref.shape[0]):
-            rows_ref[copy, tower, :, width:] = record
+    is_image = pl.program_id(0) == 0
+    acts = jnp.where(is_image, image_ref[...], text_ref[...])
+    gains = jnp.where(is_image, ig_ref[...], tg_ref[...]).reshape(1, width)
+    offset = jnp.where(is_image, io_ref[...], to_ref[...]).reshape(1, width)
+    values = acts.astype(jnp.float32)
+    row_mean = jnp.mean(values, axis=-1, keepdims=True)
+    centered = values - row_mean
+    row_var = jnp.mean(centered * centered, axis=-1, keepdims=True)
+    inverse_std = lax.rsqrt(row_var + norm_eps)
+    hat = centered * inverse_std
+    scaled = hat * gains + offset
+    inverse_len = lax.rsqrt(jnp.sum(scaled * scaled, axis=-1, keepdims=True) + unit_eps)
+    unit = scaled * inverse_len
+    along = unit * gains
+    mean_along = jnp.mean(along, axis=-1, keepdims=True)
+    mean_along_hat = jnp.mean(along * hat, axis=-1, keepdims=True)
+    unit_ref[...] = (unit * carry_scale).astype(jnp.bfloat16)
+    lane = lax.broadcasted_iota(jnp.int32, (acts.shape[0], lanes), 1)
+    record = jnp.zeros((acts.shape[0], lanes), jnp.float32)
+    index = 0
+    for stat in (row_mean, inverse_std, inverse_len, mean_along, mean_along_hat):
+        for part in split_three(stat):
+            record = jnp.where(lane == index, part, record)
+            index += 1
+    record = record.astype(jnp.bfloat16)
+    for copy in range(rows_ref.shape[0]):
+        rows_ref[copy, :, :width] = acts
+        rows_ref[copy, :, width:] = record
 
 
 def prepare(copies, image_acts, text_acts, *vectors):
     rows, width = image_acts.shape
+    acts_spec = pl.BlockSpec((rows, width), lambda t: (0, 0))
+    vector = pl.BlockSpec((width,), lambda t: (0,))
     return pl.pallas_call(
         prepare_kernel,
+        grid=(2,),
         out_shape=(
             jax.ShapeDtypeStruct((2, rows, width), jnp.bfloat16),
             jax.ShapeDtypeStruct((copies, 2, rows, width + lanes), jnp.bfloat16),
+        ),
+        in_specs=[acts_spec, acts_spec, vector, vector, vector, vector],
+        out_specs=(
+            pl.BlockSpec((None, rows, width), lambda t: (t, 0, 0)),
+            pl.BlockSpec((copies, None, rows, width + lanes), lambda t: (0, t, 0, 0)),
         ),
     )(image_acts, text_acts, *vectors)
 
@@ -105,8 +111,6 @@
         copy.start()
     vectors = ((ig_ref, io_ref), (tg_ref, to_ref))
     my_row, my_block = place_ref[0], place_ref[1]
-    window = lanes // group
-    pair_row = my_row // window
     spread_rows = lax.broadcasted_iota(jnp.int32, (lanes, stat_count * lanes), 0)
     spread_cols = lax.broadcasted_iota(jnp.int32, (lanes, stat_count * lanes), 1)
     spread = spread_rows // 3 == spread_cols // lanes
@@ -143,27 +147,17 @@
             unit = (hat * gains + offset) * wide(stat(slot, at, 2))
             embed[slot, at : at + chunk_rows] = unit.astype(jnp.bfloat16)
 
-    def score(slot, tower):
+    def score(slot, tower, first):
         scores = lax.dot_general(
             embed[slot], moving_rows(tower), last_last, preferred_element_type=jnp.float32
         )
-        probs[slot] = probability(scores).astype(jnp.bfloat16)
-
-    def label(tower):
-        slot = tower * (blocks // per_block) + my_block // per_block
-        start = (my_block % per_block) * group
-        rows = pl.ds(pl.multiple_of(start, group), group)
-        cols = pl.ds(pl.multiple_of(pair_row * lanes, lanes), lanes)
-        near = moving_ref[1 - tower, pl.ds(pair_row * window, window)].reshape(lanes, width)
-        scores = lax.dot_general(
-            embed[slot, rows], near, last_last, preferred_element_type=jnp.float32
-        )
-        row_index = lax.broadcasted_iota(jnp.int32, scores.shape, 0)
-        col_index = lax.broadcasted_iota(jnp.int32, scores.shape, 1)
-        own = row_index == col_index - (my_row % window) * group
+        row_index = lax.broadcasted_iota(jnp.int32, scores.shape, 0) + (first - my_block) * group
+        col_index = lax.broadcasted_iota(jnp.int32, scores.shape, 1) - my_row * group
+        inside = jnp.logical_and(col_index >= 0, col_index < group)
+        col_index = jnp.where(inside, col_index, -1 - block_rows * blocks)
         value = probability(scores)
-        value = jnp.where(own, value - 1.0, value)
-        probs[slot, rows, cols] = value.astype(jnp.bfloat16)
+        value = jnp.where(row_index == col_index, value - 1.0, value)
+        probs[slot] = value.astype(jnp.bfloat16)
 
     def collect(slot, tower):
         part[slot] = jnp.dot(probs[slot], moving_rows(tower), preferred_element_type=jnp.float32)
@@ -174,20 +168,21 @@
         gains_two = gains * gains
         gains_offset = gains * offset
         for block, start, at in chunks(first):
-            hat = hat_rows(slot, tower, block, start, at)
+            acts = fixed_ref[block, tower, start : start + chunk_rows, :width]
+            centered = acts.astype(jnp.float32) - wide(stat(slot, at, 0))
             grad = part[slot, at : at + chunk_rows]
             weighted = grad * gains
+            std, length = stat(slot, at, 1), stat(slot, at, 2)
             sum_one = jnp.sum(weighted, axis=-1, keepdims=True)
-            sum_hat = jnp.sum(weighted * hat, axis=-1, keepdims=True)
+            sum_hat = std * jnp.sum(weighted * centered, axis=-1, keepdims=True)
             sum_offset = jnp.sum(grad * offset, axis=-1, keepdims=True)
-            length = stat(slot, at, 2)
             along = length * (sum_hat + sum_offset)
             mean_one = sum_one * (1.0 / width) - along * stat(slot, at, 3)
             mean_two = sum_hat * (1.0 / width) - along * stat(slot, at, 4)
-            along = wide(along * length)
-            scale = (logit_scale * loss_weight / carry_scale) * length * stat(slot, at, 1)
-            removed = hat * (gains_two * along + wide(mean_two))
-            removed = removed + (gains_offset * along + wide(mean_one))
+            along = along * length
+            scale = (logit_scale * loss_weight / carry_scale) * length * std
+            removed = centered * (gains_two * wide(along * std) + wide(mean_two * std))
+            removed = removed + (gains_offset * wide(along) + wide(mean_one))
             value = (weighted - removed) * wide(scale)
             out_ref[ring_order[block], tower, start : start + chunk_rows] = value.astype(
                 jnp.bfloat16
@@ -199,10 +194,7 @@
     for slot, (tower, first) in enumerate(jobs):
         if first == 0:
             copies[1 - tower].wait()
-        score(slot, tower)
-    for tower in range(towers):
-        label(tower)
-    for slot, (tower, first) in enumerate(jobs):
+        score(slot, tower, first)
         collect(slot, tower)
         backward(slot, tower, first)
 

time: 128 us -> 128 us (level)
  no operation moved by 1% of the time
where the time goes in v4:
time: 128 us
  blocking collectives  104 us (81%)
  Pallas kernels  12.9 us (10%)
  starting transfers between devices  6.16 us (5%)
  other arithmetic  4.32 us (3%)
    all_gather x1, blocking collectives, body(): moving = lax.all_gather(units.astype(jnp.float16), 'row', axis=0)  70.4 us
    all_to_all x1, blocking collectives, body(): parts = lax.all_to_all(parts, 'col', 0, 0)  33.2 us
    pallas_call x1, Pallas kernels, pair_grads(): pl.pallas_call(pair_kernel, out_shape=jax.ShapeDtypeStruct((blocks, tower...  9.81 us
    all_to_all x1, starting transfers between devices, body(): fixed = lax.all_to_all(copies, 'col', 0, 0)  6.16 us
    convert_element_type x1, other arithmetic, body(): moving = moving.astype(jnp.bfloat16)  3.18 us
    pallas_call x1, Pallas kernels, prepare(): pl.pallas_call(prepare_kernel, grid=(2,), out_shape=(jax.ShapeDtypeStruct...  3.05 us
  transfers between devices with their start and end apart: 1, of which 0 were waited for; matrix products, arithmetic and copies ran while one was open for 3% of the time, Pallas kernels for 0%

profile of v4, /device:TPU:2, one launch (start us, length us, event | category | flops | bytes accessed | tf_op | source)
XLA Modules:
  0.0 127.7 jit_solution(3809589608869536030)
XLA Ops:
  0.6 3.0 %shard_map.77 = (bf16[2,64,1152]{2,1,0:T(8,128)(2,1)}, bf16[8,2,64,1280]{3,2,1,0:T(8,128)(2,1)}) custom-call(bf16[64,1152]{1,0:T(8,128)(2,1)} %image_ref.1, bf16[64,1152]{1,0:T(8,128)(2,1)} %text_ref.1, f32[1152]{0:T(1024)} %ig_ref.3, f32[1152]{0:T(1024)} %io_ref.3, f32[1152]{0:T(1024)} %tg_ref.3, f32[1152]{0:T(1024)} %to_ref.3), custom_call_target="tpu_custom_call" | custom-call | tf_op jit(solution)/shard_map/pallas_call | solution.py:69
  3.7 0.0 copy-start.4
  3.7 6.2 %all-to-all-start = ((bf16[8,2,64,1280]{3,2,1,0:T(8,128)(2,1)}), bf16[8,2,64,1280]{3,2,1,0:T(8,128)(2,1)S(1)}, u32[]{:S(2)}, u32[]{:S(2)}) async-start(bf16[8,2,64,1280]{3,2,1,0:T(8,128)(2,1)} %get-tuple-element.4), calls=%async_computation | async-start | bytes 5242880 | tf_op jit(solution)/shard_map/all_to_all | solution.py:249
  9.8 0.0 copy-done.4
  9.8 0.1 convert_element_type.92
  9.9 70.4 %all-gather.2 = f16[32,64,1152]{2,1,0:T(8,128)(2,1)S(1)} all-gather(f16[2,64,1152]{2,1,0:T(8,128)(2,1)S(1)} %convert_element_type.92), channel_id=2, replica_groups=mesh['row'=16,'col'=8,'rep'=4] {'row'}, dimensions={0}, use_global_device_ids=true | all-gather | bytes 5013504 | tf_op jit(solution)/shard_map/all_gather | solution.py:250
  80.3 0.0 copy-start
  80.3 0.0 copy-start.1
  80.3 0.0 copy-start.2
  80.3 0.0 copy-start.3
  80.4 3.2 %convert_element_type.128 = bf16[32,64,1152]{2,1,0:T(8,128)(2,1)} convert(f16[32,64,1152]{2,1,0:T(8,128)(2,1)S(1)} %all-gather.2) | non-fusion elementwise | flops 2359296 | bytes 9437184 | tf_op jit(solution)/shard_map/convert_element_type | solution.py:251
  83.5 0.1 pad_add_fusion.place_ref
  83.6 0.0 all-to-all-done.fixed_ref
  83.6 0.0 copy-done
  83.6 0.0 copy-done.1
  83.6 0.0 copy-done.2
  83.6 0.0 copy-done.3
  83.6 9.8 %shard_map.78 = bf16[8,2,64,1152]{3,2,1,0:T(8,128)(2,1)S(1)} custom-call(s32[2]{0:T(128)S(1)} %pad_add_fusion.place_ref, bf16[8,2,64,1280]{3,2,1,0:T(8,128)(2,1)S(1)} %all-to-all-done.fixed_ref, f32[1152]{0:T(1024)S(1)} %copy-done, f32[1152]{0:T(1024)S(1)} %copy-done.1, f32[1152]{0:T(1024)S(1)} %copy-done.2, f32[1152]{0:T(1024)S(1)} %copy-done.3, ...), custom_call_target="tpu_custom_call" | custom-call | flops 4831838208 | bytes 12582912 | tf_op jit(solution)/shard_map/pallas_call | solution.py:208
  93.5 33.2 %all_to_all.10 = bf16[8,2,64,1152]{3,2,1,0:T(8,128)(2,1)S(1)} all-to-all(bf16[8,2,64,1152]{3,2,1,0:T(8,128)(2,1)S(1)} %shard_map.78), channel_id=1, replica_groups=mesh['row'=16,'col'=8,'rep'=4] {'col'}, dimensions={0} | all-to-all | bytes 4718592 | tf_op jit(solution)/shard_map/all_to_all | solution.py:257
  126.7 1.0 fusion.1
Async XLA Ops:
  3.7 6.2 %copy-start.4 = (bf16[2,64,1152]{2,1,0:T(8,128)(2,1)S(1)}, bf16[2,64,1152]{2,1,0:T(8,128)(2,1)}, u32[]{:S(2)}) copy-start(bf16[2,64,1152]{2,1,0:T(8,128)(2,1)} %get-tuple-element.5) | copy-start | bytes 884740
  3.7 79.9 %all-to-all-start = ((bf16[8,2,64,1280]{3,2,1,0:T(8,128)(2,1)}), bf16[8,2,64,1280]{3,2,1,0:T(8,128)(2,1)S(1)}, u32[]{:S(2)}, u32[]{:S(2)}) async-start(bf16[8,2,64,1280]{3,2,1,0:T(8,128)(2,1)} %get-tuple-element.4), calls=%async_computation | async-start | bytes 5242880 | tf_op jit(solution)/shard_map/all_to_all | solution.py:249
  80.3 3.3 %copy-start = (f32[1152]{0:T(1024)S(1)}, f32[1152]{0:T(1024)}, u32[]{:S(2)}) copy-start(f32[1152]{0:T(1024)} %ig_ref.3) | copy-start | bytes 13828
  80.3 3.3 %copy-start.1 = (f32[1152]{0:T(1024)S(1)}, f32[1152]{0:T(1024)}, u32[]{:S(2)}) copy-start(f32[1152]{0:T(1024)} %io_ref.3) | copy-start | bytes 13828
  80.3 3.3 %copy-start.2 = (f32[1152]{0:T(1024)S(1)}, f32[1152]{0:T(1024)}, u32[]{:S(2)}) copy-start(f32[1152]{0:T(1024)} %tg_ref.3) | copy-start | bytes 13828
  80.3 3.3 %copy-start.3 = (f32[1152]{0:T(1024)S(1)}, f32[1152]{0:T(1024)}, u32[]{:S(2)}) copy-start(f32[1152]{0:T(1024)} %to_ref.3) | copy-start | bytes 13828

commit v5 on v4

--- a/solution.py
+++ b/solution.py
@@ -70,7 +70,7 @@
         prepare_kernel,
         grid=(2,),
         out_shape=(
-            jax.ShapeDtypeStruct((2, rows, width), jnp.bfloat16),
+            pltpu.VMEM((2, rows, width), jnp.bfloat16),
             jax.ShapeDtypeStruct((copies, 2, rows, width + lanes), jnp.bfloat16),
         ),
         in_specs=[acts_spec, acts_spec, vector, vector, vector, vector],
@@ -104,7 +104,7 @@
     rate = logit_scale * log2_e / carry_scale
     shift = -logit_shift * log2_e
     copies = [
-        pltpu.make_async_copy(moving_hbm.at[:, t], moving_ref.at[t], arrived.at[t])
+        pltpu.make_async_copy(moving_hbm.at[t], moving_ref.at[t], arrived.at[t])
         for t in range(towers)
     ]
     for copy in reversed(copies):
@@ -201,7 +201,7 @@
 
 def pair_grads(place, fixed, vectors, moving):
     blocks, towers, group, _ = fixed.shape
-    planes, _, _, width = moving.shape
+    _, planes, _, width = moving.shape
     columns = planes * group
     slots = towers * blocks * group // block_rows
     whole = pl.BlockSpec(memory_space=pltpu.VMEM)
@@ -247,7 +247,7 @@
     vectors = (image_gain, image_offset, text_gain, text_offset)
     units, copies = prepare(lax.axis_size("col"), image_acts, text_acts, *vectors)
     fixed = lax.all_to_all(copies, "col", 0, 0)
-    moving = lax.all_gather(units.astype(jnp.float16), "row", axis=0)
+    moving = lax.all_gather(units.astype(jnp.float16), "row", axis=1)
     moving = moving.astype(jnp.bfloat16)
     col = lax.axis_index("col")
     my_block = col

time: 128 us -> 128 us (level)
  transfers between devices with their start and end apart: 1 -> 1, of which waited for: 0 -> 0; matrix products, arithmetic and copies ran while one was open for 3% -> 2% of each run, Pallas kernels for 0% -> 0%
where the time goes in v5:
time: 128 us; the launch traced here: 127 us
  blocking collectives  104 us (81%)
  Pallas kernels  12.8 us (10%)
  starting transfers between devices  6.03 us (5%)
  other arithmetic  4.1 us (3%)
    all_gather x1, blocking collectives, body(): moving = lax.all_gather(units.astype(jnp.float16), 'row', axis=1)  70.4 us
    all_to_all x1, blocking collectives, body(): parts = lax.all_to_all(parts, 'col', 0, 0)  33.2 us
    pallas_call x1, Pallas kernels, pair_grads(): pl.pallas_call(pair_kernel, out_shape=jax.ShapeDtypeStruct((blocks, tower...  9.79 us
    all_to_all x1, starting transfers between devices, body(): fixed = lax.all_to_all(copies, 'col', 0, 0)  6.03 us
    pallas_call x1, Pallas kernels, prepare(): pl.pallas_call(prepare_kernel, grid=(2,), out_shape=(pltpu.VMEM((2, rows,...  3.03 us
    convert_element_type x1, other arithmetic, body(): moving = moving.astype(jnp.bfloat16)  2.97 us
  transfers between devices with their start and end apart: 1, of which 0 were waited for; matrix products, arithmetic and copies ran while one was open for 2% of the time, Pallas kernels for 0%

profile of v5, /device:TPU:2, one launch (start us, length us, event | category | flops | bytes accessed | tf_op | source)
XLA Modules:
  0.0 127.3 jit_solution(13685776945176066103)
XLA Ops:
  0.6 3.0 %shard_map.77 = (bf16[2,64,1152]{2,1,0:T(8,128)(2,1)S(1)}, bf16[8,2,64,1280]{3,2,1,0:T(8,128)(2,1)}) custom-call(bf16[64,1152]{1,0:T(8,128)(2,1)} %image_ref.1, bf16[64,1152]{1,0:T(8,128)(2,1)} %text_ref.1, f32[1152]{0:T(1024)} %ig_ref.3, f32[1152]{0:T(1024)} %io_ref.3, f32[1152]{0:T(1024)} %tg_ref.3, f32[1152]{0:T(1024)} %to_ref.3), custom_call_target="tpu_custom_call" | custom-call | tf_op jit(solution)/shard_map/pallas_call | solution.py:69
  3.7 6.0 %all-to-all-start = ((bf16[8,2,64,1280]{3,2,1,0:T(8,128)(2,1)}), bf16[8,2,64,1280]{3,2,1,0:T(8,128)(2,1)S(1)}, u32[]{:S(2)}, u32[]{:S(2)}) async-start(bf16[8,2,64,1280]{3,2,1,0:T(8,128)(2,1)} %get-tuple-element.4), calls=%async_computation | async-start | bytes 5242880 | tf_op jit(solution)/shard_map/all_to_all | solution.py:249
  9.7 0.1 convert_element_type.92
  9.7 70.4 %all-gather.2 = f16[2,1024,1152]{2,1,0:T(8,128)(2,1)S(1)} all-gather(f16[2,64,1152]{2,1,0:T(8,128)(2,1)S(1)} %convert_element_type.92), channel_id=2, replica_groups=mesh['row'=16,'col'=8,'rep'=4] {'row'}, dimensions={1}, use_global_device_ids=true | all-gather | bytes 5013504 | tf_op jit(solution)/shard_map/all_gather | solution.py:250
  80.2 0.0 copy-start
  80.2 0.0 copy-start.1
  80.2 0.0 copy-start.2
  80.2 0.0 copy-start.3
  80.2 3.0 %convert_element_type.128 = bf16[2,1024,1152]{2,1,0:T(8,128)(2,1)} convert(f16[2,1024,1152]{2,1,0:T(8,128)(2,1)S(1)} %all-gather.2) | non-fusion elementwise | flops 2359296 | bytes 9437184 | tf_op jit(solution)/shard_map/convert_element_type | solution.py:251
  83.2 0.1 pad_add_fusion.place_ref
  83.2 0.0 all-to-all-done.fixed_ref
  83.2 0.0 copy-done
  83.2 0.0 copy-done.1
  83.2 0.0 copy-done.2
  83.3 0.0 copy-done.3
  83.3 9.8 %shard_map.78 = bf16[8,2,64,1152]{3,2,1,0:T(8,128)(2,1)S(1)} custom-call(s32[2]{0:T(128)S(1)} %pad_add_fusion.place_ref, bf16[8,2,64,1280]{3,2,1,0:T(8,128)(2,1)S(1)} %all-to-all-done.fixed_ref, f32[1152]{0:T(1024)S(1)} %copy-done, f32[1152]{0:T(1024)S(1)} %copy-done.1, f32[1152]{0:T(1024)S(1)} %copy-done.2, f32[1152]{0:T(1024)S(1)} %copy-done.3, ...), custom_call_target="tpu_custom_call" | custom-call | flops 4831838208 | bytes 12582912 | tf_op jit(solution)/shard_map/pallas_call | solution.py:208
  93.1 33.2 %all_to_all.10 = bf16[8,2,64,1152]{3,2,1,0:T(8,128)(2,1)S(1)} all-to-all(bf16[8,2,64,1152]{3,2,1,0:T(8,128)(2,1)S(1)} %shard_map.78), channel_id=1, replica_groups=mesh['row'=16,'col'=8,'rep'=4] {'col'}, dimensions={0} | all-to-all | bytes 4718592 | tf_op jit(solution)/shard_map/all_to_all | solution.py:257
  126.3 1.0 fusion.1
Async XLA Ops:
  3.7 79.6 %all-to-all-start = ((bf16[8,2,64,1280]{3,2,1,0:T(8,128)(2,1)}), bf16[8,2,64,1280]{3,2,1,0:T(8,128)(2,1)S(1)}, u32[]{:S(2)}, u32[]{:S(2)}) async-start(bf16[8,2,64,1280]{3,2,1,0:T(8,128)(2,1)} %get-tuple-element.4), calls=%async_computation | async-start | bytes 5242880 | tf_op jit(solution)/shard_map/all_to_all | solution.py:249
  80.2 3.1 %copy-start = (f32[1152]{0:T(1024)S(1)}, f32[1152]{0:T(1024)}, u32[]{:S(2)}) copy-start(f32[1152]{0:T(1024)} %ig_ref.3) | copy-start | bytes 13828
  80.2 3.1 %copy-start.1 = (f32[1152]{0:T(1024)S(1)}, f32[1152]{0:T(1024)}, u32[]{:S(2)}) copy-start(f32[1152]{0:T(1024)} %io_ref.3) | copy-start | bytes 13828
  80.2 3.1 %copy-start.2 = (f32[1152]{0:T(1024)S(1)}, f32[1152]{0:T(1024)}, u32[]{:S(2)}) copy-start(f32[1152]{0:T(1024)} %tg_ref.3) | copy-start | bytes 13828
  80.2 3.1 %copy-start.3 = (f32[1152]{0:T(1024)S(1)}, f32[1152]{0:T(1024)}, u32[]{:S(2)}) copy-start(f32[1152]{0:T(1024)} %to_ref.3) | copy-start | bytes 13828

commit v6 on v5

--- a/solution.py
+++ b/solution.py
@@ -15,7 +15,7 @@
 log2_e = 1.4426950408889634
 carry_scale = 32768.0
 lanes = 128
-chunk_rows = 16
+chunk_rows = 32
 block_rows = 256
 stat_count = 5
 ring_order = (0, 1, 2, 3, 4, 5, 6, 7)

time: 128 us -> 128 us (level)
  no operation moved by 1% of the time
where the time goes in v6:
time: 128 us; the launch traced here: 127 us
  blocking collectives  104 us (81%)
  Pallas kernels  12.8 us (10%)
  starting transfers between devices  6.03 us (5%)
  other arithmetic  4.1 us (3%)
    all_gather x1, blocking collectives, body(): moving = lax.all_gather(units.astype(jnp.float16), 'row', axis=1)  70.4 us
    all_to_all x1, blocking collectives, body(): parts = lax.all_to_all(parts, 'col', 0, 0)  33.2 us
    pallas_call x1, Pallas kernels, pair_grads(): pl.pallas_call(pair_kernel, out_shape=jax.ShapeDtypeStruct((blocks, tower...  9.82 us
    all_to_all x1, starting transfers between devices, body(): fixed = lax.all_to_all(copies, 'col', 0, 0)  6.03 us
    pallas_call x1, Pallas kernels, prepare(): pl.pallas_call(prepare_kernel, grid=(2,), out_shape=(pltpu.VMEM((2, rows,...  3.03 us
    convert_element_type x1, other arithmetic, body(): moving = moving.astype(jnp.bfloat16)  2.97 us
  transfers between devices with their start and end apart: 1, of which 0 were waited for; matrix products, arithmetic and copies ran while one was open for 2% of the time, Pallas kernels for 0%

profile of v6, /device:TPU:2, one launch (start us, length us, event | category | flops | bytes accessed | tf_op | source)
XLA Modules:
  0.0 127.3 jit_solution(10443100269758109568)
XLA Ops:
  0.6 3.0 %shard_map.77 = (bf16[2,64,1152]{2,1,0:T(8,128)(2,1)S(1)}, bf16[8,2,64,1280]{3,2,1,0:T(8,128)(2,1)}) custom-call(bf16[64,1152]{1,0:T(8,128)(2,1)} %image_ref.1, bf16[64,1152]{1,0:T(8,128)(2,1)} %text_ref.1, f32[1152]{0:T(1024)} %ig_ref.3, f32[1152]{0:T(1024)} %io_ref.3, f32[1152]{0:T(1024)} %tg_ref.3, f32[1152]{0:T(1024)} %to_ref.3), custom_call_target="tpu_custom_call" | custom-call | tf_op jit(solution)/shard_map/pallas_call | solution.py:69
  3.7 6.0 %all-to-all-start = ((bf16[8,2,64,1280]{3,2,1,0:T(8,128)(2,1)}), bf16[8,2,64,1280]{3,2,1,0:T(8,128)(2,1)S(1)}, u32[]{:S(2)}, u32[]{:S(2)}) async-start(bf16[8,2,64,1280]{3,2,1,0:T(8,128)(2,1)} %get-tuple-element.4), calls=%async_computation | async-start | bytes 5242880 | tf_op jit(solution)/shard_map/all_to_all | solution.py:249
  9.7 0.1 convert_element_type.92
  9.7 70.4 %all-gather.2 = f16[2,1024,1152]{2,1,0:T(8,128)(2,1)S(1)} all-gather(f16[2,64,1152]{2,1,0:T(8,128)(2,1)S(1)} %convert_element_type.92), channel_id=2, replica_groups=mesh['row'=16,'col'=8,'rep'=4] {'row'}, dimensions={1}, use_global_device_ids=true | all-gather | bytes 5013504 | tf_op jit(solution)/shard_map/all_gather | solution.py:250
  80.2 0.0 copy-start
  80.2 0.0 copy-start.1
  80.2 0.0 copy-start.2
  80.2 0.0 copy-start.3
  80.2 3.0 %convert_element_type.128 = bf16[2,1024,1152]{2,1,0:T(8,128)(2,1)} convert(f16[2,1024,1152]{2,1,0:T(8,128)(2,1)S(1)} %all-gather.2) | non-fusion elementwise | flops 2359296 | bytes 9437184 | tf_op jit(solution)/shard_map/convert_element_type | solution.py:251
  83.2 0.1 pad_add_fusion.place_ref
  83.2 0.0 all-to-all-done.fixed_ref
  83.2 0.0 copy-done
  83.2 0.0 copy-done.1
  83.2 0.0 copy-done.2
  83.3 0.0 copy-done.3
  83.3 9.8 %shard_map.78 = bf16[8,2,64,1152]{3,2,1,0:T(8,128)(2,1)S(1)} custom-call(s32[2]{0:T(128)S(1)} %pad_add_fusion.place_ref, bf16[8,2,64,1280]{3,2,1,0:T(8,128)(2,1)S(1)} %all-to-all-done.fixed_ref, f32[1152]{0:T(1024)S(1)} %copy-done, f32[1152]{0:T(1024)S(1)} %copy-done.1, f32[1152]{0:T(1024)S(1)} %copy-done.2, f32[1152]{0:T(1024)S(1)} %copy-done.3, ...), custom_call_target="tpu_custom_call" | custom-call | flops 4831838208 | bytes 12582912 | tf_op jit(solution)/shard_map/pallas_call | solution.py:208
  93.1 33.2 %all_to_all.10 = bf16[8,2,64,1152]{3,2,1,0:T(8,128)(2,1)S(1)} all-to-all(bf16[8,2,64,1152]{3,2,1,0:T(8,128)(2,1)S(1)} %shard_map.78), channel_id=1, replica_groups=mesh['row'=16,'col'=8,'rep'=4] {'col'}, dimensions={0} | all-to-all | bytes 4718592 | tf_op jit(solution)/shard_map/all_to_all | solution.py:257
  126.3 1.0 fusion.1
Async XLA Ops:
  3.7 79.6 %all-to-all-start = ((bf16[8,2,64,1280]{3,2,1,0:T(8,128)(2,1)}), bf16[8,2,64,1280]{3,2,1,0:T(8,128)(2,1)S(1)}, u32[]{:S(2)}, u32[]{:S(2)}) async-start(bf16[8,2,64,1280]{3,2,1,0:T(8,128)(2,1)} %get-tuple-element.4), calls=%async_computation | async-start | bytes 5242880 | tf_op jit(solution)/shard_map/all_to_all | solution.py:249
  80.2 3.1 %copy-start = (f32[1152]{0:T(1024)S(1)}, f32[1152]{0:T(1024)}, u32[]{:S(2)}) copy-start(f32[1152]{0:T(1024)} %ig_ref.3) | copy-start | bytes 13828
  80.2 3.1 %copy-start.1 = (f32[1152]{0:T(1024)S(1)}, f32[1152]{0:T(1024)}, u32[]{:S(2)}) copy-start(f32[1152]{0:T(1024)} %io_ref.3) | copy-start | bytes 13828
  80.2 3.1 %copy-start.2 = (f32[1152]{0:T(1024)S(1)}, f32[1152]{0:T(1024)}, u32[]{:S(2)}) copy-start(f32[1152]{0:T(1024)} %tg_ref.3) | copy-start | bytes 13828
  80.2 3.1 %copy-start.3 = (f32[1152]{0:T(1024)S(1)}, f32[1152]{0:T(1024)}, u32[]{:S(2)}) copy-start(f32[1152]{0:T(1024)} %to_ref.3) | copy-start | bytes 13828
